TPU v7x, 512 devices: a whole 4x4x16 slice. The times are simulated.
512 devices in a mesh: slab: 32 (over z, core), work: 16 (over y, x).
Axes of the slice: x: 4, y: 4, z: 16, core: 2. Of those that a mesh axis runs over, the one named last changes fastest.
Arguments:
- volume: bfloat16 [1024, 24576], P(('slab', 'work')), may hold values from -6 to 6
- tissue: int32 [1024], P(('slab', 'work')), may hold values from 0 to 1, as said below
- w_first: bfloat16 [24, 1, 3, 3, 3], replicated, may hold values from -1.25 to 1.25
- w_second: bfloat16 [24, 24, 3, 3, 3], replicated, may hold values from -0.25 to 0.25
- w_down: bfloat16 [48, 24, 3, 3, 3], replicated, may hold values from -0.25 to 0.25
- w_up: bfloat16 [24, 48], replicated, may hold values from -0.875 to 0.875
- w_out: bfloat16 [3, 24], replicated, may hold values from -1.25 to 1.25
Outputs:
- boundary: bfloat16 [1024, 3, 16384], P(('slab', 'work'))
Inputs may be any that keep to these rules, and one draw needn't show every extreme that they name: Of the 32 bricks of each slab exactly half hold tissue.
All inputs are finite; a program needn't handle non-finite values.
Results may differ from a plain program's by a relative error of at most 0.0045.
Values may be sent and summed in bfloat16 or wider, within the bound.
No kernel may reach another device: no remote copies, remote signals or barrier semaphores. Data moves between devices by JAX's collectives and lax.ppermute only.
A program may use at most 128 MiB of HBM per device.

v0:
```python
import jax
import jax.numpy as jnp
from jax import lax
from jax.sharding import PartitionSpec as P

SIDE = 32
DEPTH = 16
MARGIN = 4
EXTENT = 24
CHANNELS = 24
CLASSES = 3
SLOTS = 1


def padded(array, sides, width):
    for axis, dim in sides:
        peers, length = (lax.axis_size(axis), array.shape[dim])
        up = [(i, (i + 1) % peers) for i in range(peers - 1)]
        down = [(j, i) for i, j in up]
        last = lax.slice_in_dim(array, length - width, length, axis=dim)
        first = lax.slice_in_dim(array, 0, width, axis=dim)
        before = lax.ppermute(last, axis, up)
        after = lax.ppermute(first, axis, down)
        array = jnp.concatenate([before, array, after], axis=dim)
    return array


def conv3(x, w):
    return lax.conv_general_dilated(
        x,
        w,
        (1, 1, 1),
        "SAME",
        dimension_numbers=("NCDHW", "OIDHW", "NCDHW"),
        preferred_element_type=jnp.float32,
    )


def network(bricks, w_first, w_second, w_down, w_up, w_out):
    count = bricks.shape[0]
    field = bricks.reshape(count, 1, EXTENT, SIDE, SIDE)
    first = jax.nn.relu(conv3(field, w_first)).astype(jnp.bfloat16)
    fine = jax.nn.relu(conv3(first, w_second)).astype(jnp.bfloat16)
    cubes = fine.reshape(count, CHANNELS, EXTENT // 2, 2, SIDE // 2, 2, SIDE // 2, 2)
    pooled = jnp.max(cubes, axis=(3, 5, 7))
    downsampled_features = jax.nn.relu(conv3(pooled, w_down)).astype(jnp.bfloat16)
    lifted = jnp.einsum(
        "oc,ncxyz->noxyz", w_up, downsampled_features, preferred_element_type=jnp.float32
    )
    mixed = cubes.astype(jnp.float32) + lifted[:, :, :, None, :, None, :, None]
    mixed = jax.nn.relu(mixed).astype(jnp.bfloat16).reshape(count, CHANNELS, EXTENT * SIDE * SIDE)
    logits = jnp.einsum("oc,ncv->nov", w_out, mixed, preferred_element_type=jnp.float32)
    return jax.nn.sigmoid(logits).astype(jnp.bfloat16).reshape(count, CLASSES, EXTENT, SIDE * SIDE)


def shards(volume, tissue, w_first, w_second, w_down, w_up, w_out):
    owned = volume.shape[0]
    cells = volume.shape[1]
    workers = lax.axis_size("work")
    width = cells // workers
    group_marks = lax.all_gather(tissue, "work", axis=0, tiled=True)
    before = jnp.cumsum(group_marks) - group_marks
    targets = jnp.arange(workers * SLOTS, dtype=jnp.int32)
    pick_entries = ((before[None, :] == targets[:, None]) & (group_marks[None, :] == 1)).astype(
        jnp.bfloat16
    )
    divide_into_bricks = volume.reshape(owned, workers, width)
    columns = lax.all_to_all(divide_into_bricks, "work", split_axis=1, concat_axis=0, tiled=True)
    columns = columns.reshape(workers * owned, width)
    picked_slots = jnp.dot(pick_entries, columns, preferred_element_type=jnp.float32).astype(
        jnp.bfloat16
    )
    picked_slots = picked_slots.reshape(workers, SLOTS, width)
    received_pieces = lax.all_to_all(picked_slots, "work", split_axis=0, concat_axis=0, tiled=True)
    count = received_pieces.shape[1]
    whole = jnp.transpose(received_pieces, (1, 0, 2)).reshape(count, cells)
    results = network(whole, w_first, w_second, w_down, w_up, w_out)
    results = results.reshape(SLOTS, CLASSES, workers, width)
    results = jnp.transpose(results, (1, 0, 2, 3)).reshape(CLASSES, SLOTS * workers, width)
    collected_rows = lax.all_to_all(results, "work", split_axis=1, concat_axis=1, tiled=True)
    scatter_pieces = jnp.einsum(
        "nh,lnv->hlv", pick_entries, collected_rows, preferred_element_type=jnp.float32
    ).astype(jnp.bfloat16)
    scatter_pieces = scatter_pieces.reshape(workers, owned, CLASSES, 1, width)
    returned = lax.all_to_all(scatter_pieces, "work", split_axis=0, concat_axis=3, tiled=True)
    preds = returned.reshape(owned, CLASSES, EXTENT, SIDE * SIDE)
    border_extended = padded(preds, (("slab", 2),), MARGIN)
    core = border_extended[:, :, 2 * MARGIN : 2 * MARGIN + DEPTH].astype(jnp.float32)
    from_below = border_extended[:, :, :MARGIN].astype(jnp.float32)
    from_above = border_extended[:, :, EXTENT + MARGIN :].astype(jnp.float32)
    total = core + jnp.pad(from_below, ((0, 0), (0, 0), (0, DEPTH - MARGIN), (0, 0)))
    total = total + jnp.pad(from_above, ((0, 0), (0, 0), (DEPTH - MARGIN, 0), (0, 0)))
    return total.astype(jnp.bfloat16).reshape(owned, CLASSES, DEPTH * SIDE * SIDE)


def solution(mesh):
    return jax.shard_map(
        shards,
        mesh=mesh,
        in_specs=(P(("slab", "work"), None), P(("slab", "work")), P(), P(), P(), P(), P()),
        out_specs=P(("slab", "work"), None, None),
        check_vma=False,
    )
```

profile of v0, /device:TPU:1, one launch (start us, length us, event | category | flops | bytes accessed | tf_op | source)
XLA Modules:
  0.0 213.0 jit_solution(2573147871156974013)
XLA Ops:
  0.0 7.7 %all-to-all-start = ((bf16[2,16,1536]{2,0,1:T(2,128)(2,1)}), bf16[2,16,1536]{2,0,1:T(2,128)(2,1)S(1)}, u32[]{:S(2)}, u32[]{:S(2)}) async-start(bf16[2,16,1536]{2,0,1:T(2,128)(2,1)} %bitcast.93), calls=%async_computation | async-start | bytes 196608 | tf_op jit(solution)/shard_map/all_to_all | solution.py:68
  7.8 1.3 dynamic-slice
  9.7 0.9 dynamic-update-slice
  10.5 12.9 %all-reduce.2 = s32[32]{0:T(128)S(1)} all-reduce(s32[32]{0:T(128)S(1)} %dynamic-update-slice), channel_id=1, replica_groups=mesh['slab'=32,'work'=16] {'work'}, use_global_device_ids=true, to_apply=%add.2 | all-reduce | flops 32 | bytes 256
  25.1 9.1 %all_to_all.40 = bf16[16,2,768]{2,1,0:T(2,128)(2,1)S(1)} all-to-all(bf16[16,2,768]{2,1,0:T(2,128)(2,1)S(1)} %reshape.129), channel_id=1, replica_groups=mesh['slab'=32,'work'=16] {'work'}, dimensions={0} | all-to-all | bytes 98304 | tf_op jit(solution)/shard_map/all_to_all | solution.py:74
  35.0 4.2 %copy.86 = bf16[1,24,32,8,7]{3,0,4,2,1:T(2,128)(2,1)S(1)} copy(bf16[1,24,32,8,7]{2,1,4,3,0:T(8,128)(2,1)S(1)} %fusion.35) | data formatting | bytes 172032 | tf_op jit(solution)/shard_map/conv_general_dilated | solution.py:29
  39.2 25.2 %select_bitcast_fusion = bf16[24,32,1,8,5,24]{5,3,4,1,0,2:T(8,128)(2,1)S(1)} fusion(bf16[1,24,32,8,7]{3,0,4,2,1:T(2,128)(2,1)S(1)} %copy.86, pred[8,5]{0,1:T(8,128)(4,1)S(1)} %copy-done.10, bf16[24,1,3,3,3]{0,4,3,2,1:T(4,128)(2,1)S(1)} %copy-done.9), kind=kOutput, calls=%fused_computation.20 | convolution fusion | flops 40849920 | bytes 1561912 | tf_op jit(solution)/shard_map/conv_general_dilated | solution.py:29
  65.1 24.6 %maximum_convert_fusion = bf16[24,32,8,5,24]{4,2,3,1,0:T(8,128)(2,1)} fusion(bf16[24,24,3,3,3]{1,0,4,3,2:T(8,128)(2,1)S(1)} %copy-done, bf16[24,32,1,7,1,24]{5,3,4,1,0,2:T(8,128)(2,1)S(1)} %get-tuple-element.6, bf16[24,32,1,7,1,24]{5,3,4,1,0,2:T(8,128)(2,1)S(1)} %get-tuple-element.5, bf16[24,32,1,8,5,24]{5,3,4,1,0,2:T(8,128)(2,1)S(1)} %select_bitcast_fusion), kind=kOutput, calls=%fused_computation.9 | convolution fusion | flops 921415680 | bytes 3496320 | tf_op jit(solution)/shard_map/conv_general_dilated | solution.py:29
  89.7 10.3 %copy.88 = bf16[24,32,8,5,24]{1,4,3,2,0:T(8,128)(2,1)} copy(bf16[24,32,8,5,24]{4,2,3,1,0:T(8,128)(2,1)} %maximum_convert_fusion) | data formatting | bytes 2949120 | tf_op jit(solution)/shard_map/convert_element_type | solution.py:43
  100.0 9.1 %slice_bitcast_fusion = (bf16[1,24,24,32,32]{3,1,4,2,0:T(8,128)(2,1)}, f32[1,24,24,32,32]{3,1,4,2,0:T(8,128)}) fusion(bf16[24,32,1,40,24]{1,4,3,0,2:T(8,128)(2,1)} %bitcast.84), kind=kLoop, calls=%fused_computation.22 | loop fusion | flops 589824 | bytes 4718592 | tf_op jit(solution)/shard_map/convert_element_type | solution.py:43
  109.2 11.6 %copy.90 = bf16[1,24,24,32,32]{1,4,3,2,0:T(8,128)(2,1)} copy(bf16[1,24,24,32,32]{3,1,4,2,0:T(8,128)(2,1)} %get-tuple-element.7) | data formatting | bytes 2359296 | tf_op jit(solution)/shard_map/convert_element_type | solution.py:43
  120.8 12.1 %reduce_max.11 = bf16[24,12,16,16]{0,3,2,1:T(8,128)(2,1)S(1)} reduce(bf16[24,12,2,16,2,16,2]{0,6,5,4,3,2,1:T(2,128)(2,1)} %bitcast.83, bf16[]{:T(256)} %constant.20.clone.1), dimensions={2,4,6}, to_apply=%region_1.2 | reduce | flops 516096 | bytes 1327106 | tf_op jit(solution)/shard_map/reduce_max | solution.py:45
  134.0 3.7 %maximum_convert_fusion.2 = bf16[12,16,8,3,48]{4,2,3,1,0:T(8,128)(2,1)S(1)} fusion(bf16[48,24,3,3,3]{0,1,4,3,2:T(8,128)(2,1)S(1)} %copy-done.8, bf16[24,12,16,1,7,2]{0,4,5,2,1,3:T(8,128)(2,1)S(1)} %slice.22, bf16[24,12,16,1,8,3]{0,4,5,2,1,3:T(8,128)(2,1)S(1)} %copy.93, pred[8,3]{0,1:T(4,128)(4,1)S(1)} %copy-done.11), kind=kOutput, calls=%fused_computation.25 | convolution fusion | flops 261218304 | bytes 854808 | tf_op jit(solution)/shard_map/conv_general_dilated | solution.py:29
  138.1 9.6 %copy.89 = f32[1,24,24,32,32]{4,3,2,1,0:T(8,128)} copy(f32[1,24,24,32,32]{3,1,4,2,0:T(8,128)} %get-tuple-element.8) | data formatting | bytes 4718592 | tf_op jit(solution)/shard_map/convert_element_type | solution.py:50
  147.7 7.8 %reshape.106 = f32[24,24576]{1,0:T(8,128)} reshape(f32[1,24,24,32,32]{4,3,2,1,0:T(8,128)} %copy.89) | data formatting | bytes 4718592 | tf_op jit(solution)/shard_map/convert_element_type | solution.py:50
  155.8 7.3 %add.34 = f32[24,12,2,16,2,16,2]{0,6,5,4,3,2,1:T(2,128)} broadcast(f32[24,12,16,16]{0,3,2,1:T(8,128)S(1)} %convolution_bitcast_fusion), dimensions={0,1,3,5} | broadcast | bytes 2654208 | tf_op jit(solution)/shard_map/add | solution.py:50
  163.1 7.7 %copy.96 = f32[24,24576]{1,0:T(8,128)S(1)} copy(f32[24,24576]{0,1:T(8,128)} %bitcast.82) | data formatting | bytes 4718592 | tf_op jit(solution)/shard_map/add | solution.py:50
  170.9 2.2 %fusion.3 = bf16[24576,3]{0,1:T(4,128)(2,1)S(1)} fusion(bf16[3,24]{1,0:T(4,128)(2,1)S(1)} %copy-done.7, f32[24,24576]{1,0:T(8,128)} %reshape.106, f32[24,24576]{1,0:T(8,128)S(1)} %copy.96), kind=kOutput, calls=%fused_computation.4 | convolution fusion | flops 5603328 | bytes 4866192 | tf_op jit(solution)/shard_map/oc,ncv->nov/dot_general | solution.py:52
  173.1 10.0 %all_to_all.41 = bf16[3,16,1536]{2,0,1:T(4,128)(2,1)S(1)} all-to-all(bf16[3,16,1536]{2,0,1:T(4,128)(2,1)S(1)} %bitcast.91), channel_id=1, replica_groups=mesh['slab'=32,'work'=16] {'work'}, dimensions={1} | all-to-all | bytes 294912 | tf_op jit(solution)/shard_map/all_to_all | solution.py:80
  183.8 10.4 %all_to_all.42 = bf16[16,2,3,1,1536]{4,1,3,2,0:T(2,128)(2,1)S(1)} all-to-all(bf16[16,2,3,1,1536]{4,1,3,2,0:T(2,128)(2,1)S(1)} %copy.99), channel_id=1, replica_groups=mesh['slab'=32,'work'=16] {'work'}, dimensions={0} | all-to-all | bytes 589824 | tf_op jit(solution)/shard_map/all_to_all | solution.py:85
  194.5 12.1 %collective-permute-start = (bf16[2,3,4,1024]{3,2,1,0:T(4,128)(2,1)S(1)}, bf16[2,3,4,1024]{3,2,1,0:T(4,128)(2,1)S(1)}, u32[]{:S(2)}, u32[]{:S(2)}) collective-permute-start(bf16[2,3,4,1024]{3,2,1,0:T(4,128)(2,1)S(1)} %get-tuple-element.9), channel_id=1, source_target_pairs={{0,16},{16,32},{32,48},{48,64},{64,80},{80,96},{96,112},{112,128},... | collective-permute-start | bytes 147464 | tf_op jit(solution)/shard_map/ppermute | solution.py:22
  206.6 1.9 collective-permute-start.1
  208.5 3.5 %collective-permute-done.1 = bf16[2,3,4,1024]{3,2,1,0:T(4,128)(2,1)S(1)} collective-permute-done((bf16[2,3,4,1024]{3,2,1,0:T(4,128)(2,1)S(1)}, bf16[2,3,4,1024]{3,2,1,0:T(4,128)(2,1)S(1)}, u32[]{:S(2)}, u32[]{:S(2)}) %collective-permute-start.1) | collective-permute-done | bytes 49184 | tf_op jit(solution)/shard_map/ppermute | solution.py:23
  212.1 0.8 reshape.88
  (60 shorter events, 5.8 us)
Async XLA Ops:
  0.0 65.1 %copy-start = (bf16[24,24,3,3,3]{1,0,4,3,2:T(8,128)(2,1)S(1)}, bf16[24,24,3,3,3]{1,0,4,3,2:T(8,128)(2,1)}, u32[]{:S(2)}) copy-start(bf16[24,24,3,3,3]{1,0,4,3,2:T(8,128)(2,1)} %param.10) | copy-start | bytes 93316
  0.0 39.2 %copy-start.10 = (pred[8,5]{0,1:T(8,128)(4,1)S(1)}, pred[8,5]{0,1:T(8,128)(4,1)}, u32[]{:S(2)}) copy-start(pred[8,5]{0,1:T(8,128)(4,1)} %constant.39) | copy-start | bytes 124
  0.0 39.2 %copy-start.9 = (bf16[24,1,3,3,3]{0,4,3,2,1:T(4,128)(2,1)S(1)}, bf16[24,1,3,3,3]{0,4,3,2,1:T(4,128)(2,1)}, u32[]{:S(2)}) copy-start(bf16[24,1,3,3,3]{0,4,3,2,1:T(4,128)(2,1)} %param.9) | copy-start | bytes 3892
  0.0 23.7 %all-to-all-start = ((bf16[2,16,1536]{2,0,1:T(2,128)(2,1)}), bf16[2,16,1536]{2,0,1:T(2,128)(2,1)S(1)}, u32[]{:S(2)}, u32[]{:S(2)}) async-start(bf16[2,16,1536]{2,0,1:T(2,128)(2,1)} %bitcast.93), calls=%async_computation | async-start | bytes 196608 | tf_op jit(solution)/shard_map/all_to_all | solution.py:68
  23.4 10.8 %copy-start.3 = (pred[32]{0:T(512)(128)(4,1)}, pred[32]{0:T(512)(128)(4,1)S(1)}, u32[]{:S(2)}) copy-start(pred[32]{0:T(512)(128)(4,1)S(1)} %broadcast_compare_fusion) | copy-start | bytes 100
  23.7 10.6 %copy-start.5 = (s32[32]{0:T(128)}, s32[32]{0:T(128)S(1)}, u32[]{:S(2)}) copy-start(s32[32]{0:T(128)S(1)} %sub.3) | copy-start | bytes 388
  132.9 1.0 copy-start.8
  132.9 1.0 copy-start.11
  147.7 7.8 %copy-start.2 = (bf16[24,48]{1,0:T(8,128)(2,1)S(1)}, bf16[24,48]{1,0:T(8,128)(2,1)}, u32[]{:S(2)}) copy-start(bf16[24,48]{1,0:T(8,128)(2,1)} %param.12) | copy-start | bytes 6916
  163.1 7.7 %copy-start.7 = (bf16[3,24]{1,0:T(4,128)(2,1)S(1)}, bf16[3,24]{1,0:T(4,128)(2,1)}, u32[]{:S(2)}) copy-start(bf16[3,24]{1,0:T(4,128)(2,1)} %param.13) | copy-start | bytes 436
  163.1 49.8 %copy-start.1 = (bf16[24,24,3,3,3]{1,0,4,3,2:T(8,128)(2,1)S(1)}, bf16[24,24,3,3,3]{1,0,4,3,2:T(8,128)(2,1)}, u32[]{:S(2)}) copy-start(bf16[24,24,3,3,3]{1,0,4,3,2:T(8,128)(2,1)} %param.10) | copy-start | bytes 93316
  170.8 12.3 %copy-start.4 = (pred[32]{0:T(512)(128)(4,1)S(1)}, pred[32]{0:T(512)(128)(4,1)}, u32[]{:S(2)}) copy-start(pred[32]{0:T(512)(128)(4,1)} %copy-done.3) | copy-start | bytes 100
  170.9 12.3 %copy-start.6 = (s32[32]{0:T(128)S(1)}, s32[32]{0:T(128)}, u32[]{:S(2)}) copy-start(s32[32]{0:T(128)} %copy-done.5) | copy-start | bytes 388
  194.5 14.1 %collective-permute-start = (bf16[2,3,4,1024]{3,2,1,0:T(4,128)(2,1)S(1)}, bf16[2,3,4,1024]{3,2,1,0:T(4,128)(2,1)S(1)}, u32[]{:S(2)}, u32[]{:S(2)}) collective-permute-start(bf16[2,3,4,1024]{3,2,1,0:T(4,128)(2,1)S(1)} %get-tuple-element.9), channel_id=1, source_target_pairs={{0,16},{16,32},{32,48},{48,64},{64,80},{80,96},{96,112},{112,128},... | collective-permute-start | bytes 147464 | tf_op jit(solution)/shard_map/ppermute | solution.py:22
  206.6 5.4 %collective-permute-start.1 = (bf16[2,3,4,1024]{3,2,1,0:T(4,128)(2,1)S(1)}, bf16[2,3,4,1024]{3,2,1,0:T(4,128)(2,1)S(1)}, u32[]{:S(2)}, u32[]{:S(2)}) collective-permute-start(bf16[2,3,4,1024]{3,2,1,0:T(4,128)(2,1)S(1)} %get-tuple-element.10), channel_id=1, source_target_pairs={{16,0},{32,16},{48,32},{64,48},{80,64},{96,80},{112,96},{128,112},... | collective-permute-start | bytes 147464 | tf_op jit(solution)/shard_map/ppermute | solution.py:23
where the time goes:
time: 216 us; the launch traced here: 213 us
  local copies, waits for them, and re-layouts  65.1 us (30%)
  matrix products  56.5 us (26%)
  blocking collectives  42.4 us (20%)
  other arithmetic  22.6 us (10%)
  starting transfers between devices  21.8 us (10%)
  waiting for transfers between devices  3.48 us (2%)
    conv_general_dilated x3, matrix products, conv3(): lax.conv_general_dilated(x, w, (1, 1, 1), 'SAME', dimension_numbers=('NCD...  53.5 us
    convert_element_type x2, local copies, waits for them, and re-layouts, network(): fine = jax.nn.relu(conv3(first, w_second)).astype(jnp.bfloat16)  21.9 us
    convert_element_type x2, local copies, waits for them, and re-layouts, network(): mixed = cubes.astype(jnp.float32) + lifted[:, :, :, None, :, None, :, None]  17.4 us
    add x2, local copies, waits for them, and re-layouts, network(): mixed = cubes.astype(jnp.float32) + lifted[:, :, :, None, :, None, :, None]  15 us
    unnamed x1, blocking collectives  12.9 us
    reduce_max x1, other arithmetic, network(): pooled = jnp.max(cubes, axis=(3, 5, 7))  12.1 us
    ppermute x1, starting transfers between devices, padded(): before = lax.ppermute(last, axis, up)  12.1 us
    all_to_all x1, blocking collectives, shards(): lax.all_to_all(scatter_pieces, 'work', split_axis=0, concat_axis=3, tiled...  10.4 us
  transfers between devices with their start and end apart: 3, of which 1 were waited for; matrix products, arithmetic and copies ran while one was open for 1% of the time, Pallas kernels for 0%

commit v1 on v0

v1 whole, which is shorter than its diff:
```python
import functools

import jax
import jax.numpy as jnp
from jax import lax
from jax.experimental import pallas as pl
from jax.experimental.pallas import tpu as pltpu
from jax.sharding import PartitionSpec as P

SIDE = 32
DEPTH = 16
MARGIN = 4
EXTENT = 24
CHANNELS = 24
COARSE = 48
CLASSES = 3
OWNED = 2
HALF = EXTENT // 2
LANES = 256
PLANE = SIDE * SIDE
VROWS = 48
HROWS = 16 * CHANNELS
PROWS = 224
BIG = -1e30

f32 = jnp.float32
bf16 = jnp.bfloat16


def dot(a, b):
    return jnp.dot(a, b, preferred_element_type=f32)


def iota(shape, dim):
    return lax.broadcasted_iota(jnp.int32, shape, dim)


def shifted(x, sy, sx, yy, xx):
    if sx:
        x = pltpu.roll(x, (-sx) % LANES, 1)
        x = jnp.where(xx == (15 if sx > 0 else 0), 0.0, x)
    if sy:
        x = pltpu.roll(x, (-16 * sy) % LANES, 1)
        x = jnp.where(yy == (15 if sy > 0 else 0), 0.0, x)
    return x


def swap_chunks(parts, low):
    out = []
    for j in range(4):
        halves = []
        for d in range(2):
            piece = [parts[2 * d + i][:, 128 * (j // 2) : 128 * (j // 2) + 128] for i in range(2)]
            if j % 2 == 0:
                halves.append(jnp.where(low, piece[0], pltpu.roll(piece[1], 64, 1)))
            else:
                halves.append(jnp.where(low, pltpu.roll(piece[0], 64, 1), piece[1]))
        out.append(jnp.concatenate(halves, axis=1))
    return out


def unet(
    tissue, vol, w1, w2, wd, wup, wout,
    core, low_out, high_out,
    t1, b2, td, w1big, w2big, wd3, wo, vs, vz, hx, fs, ys, rs,
):
    lane = iota((1, LANES), 1)
    yy, xx = lane >> 4, lane & 15
    low64 = iota((1, 128), 1) < 64

    t1[...] = jnp.zeros_like(t1)
    for kz in range(3):
        for ky in range(3):
            t1[kz * 48 + ky * 8 : kz * 48 + ky * 8 + 3, 0:CHANNELS] = w1[kz * 3 + ky].astype(f32)
    base1 = t1[...].T[0:CHANNELS]
    for pz in range(2):
        for ey in range(4):
            for half in range(2):
                rows = []
                for ex in (2 * half, 2 * half + 1):
                    s = pz * 48 + ey * 8 + ex
                    m = pltpu.roll(base1, s, 1) if s else base1
                    for on, col in ((ey == 0, 6), (ey == 3, 7), (ex == 0, 14), (ex == 3, 15)):
                        if on:
                            m = jnp.where(lane == col, BIG, m)
                    rows.append(m)
                at = (pz * 16 + ey * 4 + 2 * half) * CHANNELS
                w1big[at : at + 48] = jnp.concatenate(rows, axis=0)[:, 0:192].astype(bf16)

    b2[...] = jnp.zeros_like(b2)
    for kz in range(3):
        for ky in range(3):
            at = kz * HROWS + ky * 96
            b2[:, at : at + 72] = jnp.concatenate(
                [w2[kz * 9 + ky * 3 + kx].astype(f32) for kx in range(3)], axis=1
            )
    base2 = b2[...]
    for oz in range(2):
        for oy in range(2):
            rows = []
            for ox in range(2):
                s = oz * HROWS + oy * 96 + ox * 24
                rows.append(pltpu.roll(base2, s, 1) if s else base2)
            at = (oz * 4 + oy * 2) * CHANNELS
            w2big[at : at + 48] = jnp.concatenate(rows, axis=0).astype(bf16)

    td[...] = jnp.zeros_like(td)
    for kz in range(3):
        for k in range(9):
            td[kz, k * 24 : k * 24 + 24, 0:COARSE] = wd[kz * 9 + k].astype(f32)
    for kz in range(3):
        wd3[kz * COARSE : kz * COARSE + COARSE] = td[kz].T[0:COARSE, 0:PROWS].astype(bf16)

    ci = iota((CHANNELS, 192), 0)
    col = iota((CHANNELS, 192), 1)
    tiled = dot(wout[...], (col % 24 == ci).astype(bf16))
    r = iota((32, 192), 0)
    c = iota((32, 192), 1) // 24
    acc = jnp.zeros((32, 192), f32)
    for cls in range(CLASSES):
        acc = acc + jnp.where((r & 3) == cls, tiled[cls : cls + 1], 0.0)
    wo[...] = jnp.where(c == ((r >> 2) & 1) * 4 + (r >> 3), acc, 0.0).astype(bf16)

    def source(l):
        p = l >> 6
        return ((l >> 4) & 3) * 64 + (p >> 1) * 32 + (l & 15) * 2 + (p & 1)

    sort = (iota((LANES, LANES), 0) == source(lane)).astype(bf16)
    unsort = (iota((LANES, LANES), 1) == source(iota((LANES, 1), 0))).astype(bf16)

    for z in range(EXTENT):
        for t in range(4):
            at = z * PLANE + t * LANES
            for d in range(2):
                vs[d, pl.ds(t * EXTENT + z, OWNED, stride=96), :] = vol[
                    :, at + 128 * d : at + 128 * d + 128
                ].astype(f32)
    sorted_cells = dot(jnp.concatenate([vs[0], vs[1]], axis=1).astype(bf16), sort)
    zero_plane = jnp.zeros((VROWS, LANES), f32)
    for b in range(OWNED):
        vz[b] = jnp.zeros((2, 26 * VROWS, 128), f32)
        parts = [sorted_cells[b * 96 + t * 24 : b * 96 + t * 24 + 24] for t in range(4)]
        parities = swap_chunks(parts, low64)
        for p in range(4):
            for sy in (-1, 0, 1):
                for sx in (-1, 0, 1):
                    row = (2 * sy + (p >> 1) + 2) * 8 + 2 * sx + (p & 1) + 2
                    near = shifted(parities[p], sy, sx, yy, xx)
                    for d in range(2):
                        vz[b, d, pl.ds(VROWS + row, EXTENT, stride=VROWS), :] = near[
                            :, 128 * d : 128 * d + 128
                        ]
        for row, m in ((6, yy == 0), (7, yy == 15), (14, xx == 0), (15, xx == 15)):
            for d in range(2):
                vz[b, d, pl.ds(row, 26, stride=VROWS), :] = jnp.broadcast_to(
                    m[:, 128 * d : 128 * d + 128].astype(f32), (26, 128)
                )
        hx[b, 0:HROWS] = jnp.zeros((HROWS, LANES), bf16)
        hx[b, 25 * HROWS : 26 * HROWS] = jnp.zeros((HROWS, LANES), bf16)
        ys[b, 0] = jnp.zeros((144, LANES), f32)
        ys[b, HALF + 1] = jnp.zeros((144, LANES), f32)

    def first(i, carry):
        for b in range(OWNED):
            at = pl.multiple_of(i * (2 * VROWS), 2 * VROWS)
            near = [vz[b, d, pl.ds(at, 4 * VROWS), :] for d in range(2)]
            near = jnp.concatenate(near, axis=1).astype(bf16)
            out = jnp.maximum(dot(w1big[...], near), 0.0).astype(bf16)
            to = pl.multiple_of(i * (2 * HROWS), HROWS) + HROWS
            hx[b, pl.ds(pl.multiple_of(to, HROWS), 2 * HROWS), :] = out
        return carry

    lax.fori_loop(0, HALF, first, 0)

    def second(i, carry):
        for b in range(OWNED):
            at = pl.multiple_of(i * (2 * HROWS), 2 * HROWS)
            fine = jnp.maximum(dot(w2big[...], hx[b, pl.ds(at, 4 * HROWS), :]), 0.0)
            fs[b, i] = fine.astype(bf16)
            p = functools.reduce(jnp.maximum, [fine[c * 24 : c * 24 + 24] for c in range(8)])
            near = [shifted(p, sy, sx, yy, xx) for sy in (-1, 0, 1) for sx in (-1, 0, 1)]
            near = jnp.concatenate(near + [jnp.zeros((8, LANES), f32)], axis=0).astype(bf16)
            ys[b, i + 1] = dot(wd3[...], near)
        return carry

    lax.fori_loop(0, HALF, second, 0)

    def third(i, carry):
        for b in range(OWNED):
            g = ys[b, i, 0:48] + ys[b, i + 1, 48:96] + ys[b, i + 2, 96:144]
            u = dot(wup[...], jnp.maximum(g, 0.0).astype(bf16))
            fine = fs[b, i].astype(f32).reshape(8, CHANNELS, LANES)
            z = jnp.maximum(fine + u[None], 0.0).reshape(8 * CHANNELS, LANES).astype(bf16)
            pred = jax.nn.sigmoid(dot(wo[...], z))
            pred = jnp.where(tissue[b] == 1, pred, 0.0)
            at = pl.multiple_of(i * 8, 8)
            for p in range(4):
                rs[b, p, pl.ds(at, 8), :] = pred[p * 8 : p * 8 + 8]
        return carry

    lax.fori_loop(0, HALF, third, 0)

    for b in range(OWNED):
        chunks = swap_chunks([rs[b, p] for p in range(4)], low64)
        for t in range(4):
            rows = dot(chunks[t].astype(bf16), unsort).astype(bf16)
            rows = rows.astype(f32)
            for z in range(EXTENT):
                at = (z // 2) * 8 + (z % 2) * 4
                piece = rows[at : at + CLASSES].astype(bf16)
                if z < MARGIN:
                    to, ref = z, low_out
                elif z < MARGIN + DEPTH:
                    to, ref = z - MARGIN, core
                else:
                    to, ref = z - MARGIN - DEPTH, high_out
                ref[b, :, to * PLANE + t * LANES : to * PLANE + t * LANES + LANES] = piece


def border_sum(core, below, above, out):
    edge = MARGIN * PLANE
    full = DEPTH * PLANE
    out[:, :, edge : full - edge] = core[:, :, edge : full - edge]
    out[:, :, 0:edge] = (core[:, :, 0:edge].astype(f32) + below[...].astype(f32)).astype(bf16)
    out[:, :, full - edge :] = (
        core[:, :, full - edge :].astype(f32) + above[...].astype(f32)
    ).astype(bf16)


VMEM = pl.BlockSpec(memory_space=pltpu.VMEM)
SMEM = pl.BlockSpec(memory_space=pltpu.SMEM)


def evaluate(volume, tissue, w_first, w_second, w_down, w_up, w_out):
    w1 = jnp.transpose(w_first, (1, 2, 3, 4, 0)).reshape(9, 3, CHANNELS)
    w2 = jnp.transpose(w_second, (2, 3, 4, 0, 1)).reshape(27, CHANNELS, CHANNELS)
    wd = jnp.transpose(w_down, (2, 3, 4, 1, 0)).reshape(27, CHANNELS, COARSE)
    edge = jax.ShapeDtypeStruct((OWNED, CLASSES, MARGIN * PLANE), bf16)
    return pl.pallas_call(
        unet,
        out_shape=(jax.ShapeDtypeStruct((OWNED, CLASSES, DEPTH * PLANE), bf16), edge, edge),
        in_specs=[SMEM] + [VMEM] * 6,
        out_specs=(VMEM,) * 3,
        scratch_shapes=[
            pltpu.VMEM((256, 128), f32),
            pltpu.VMEM((CHANNELS, 4 * HROWS), f32),
            pltpu.VMEM((3, 256, 128), f32),
            pltpu.VMEM((2 * HROWS, 192), bf16),
            pltpu.VMEM((192, 4 * HROWS), bf16),
            pltpu.VMEM((144, PROWS), bf16),
            pltpu.VMEM((32, 192), bf16),
            pltpu.VMEM((2, 192, 128), f32),
            pltpu.VMEM((OWNED, 2, 26 * VROWS, 128), f32),
            pltpu.VMEM((OWNED, 26 * HROWS, LANES), bf16),
            pltpu.VMEM((OWNED, HALF, 192, LANES), bf16),
            pltpu.VMEM((OWNED, HALF + 2, 144, LANES), f32),
            pltpu.VMEM((OWNED, 4, HALF * 8, LANES), f32),
        ],
        compiler_params=pltpu.CompilerParams(vmem_limit_bytes=48 << 20),
    )(tissue, volume, w1, w2, wd, w_up, w_out)


def shards(volume, tissue, w_first, w_second, w_down, w_up, w_out):
    core, low, high = evaluate(volume, tissue, w_first, w_second, w_down, w_up, w_out)
    slabs = lax.axis_size("slab")
    up = [(i, i + 1) for i in range(slabs - 1)]
    down = [(i + 1, i) for i in range(slabs - 1)]
    below = lax.ppermute(high, "slab", up)
    above = lax.ppermute(low, "slab", down)
    return pl.pallas_call(
        border_sum,
        out_shape=jax.ShapeDtypeStruct(core.shape, bf16),
        in_specs=[VMEM] * 3,
        out_specs=VMEM,
    )(core, below, above)


def solution(mesh):
    return jax.shard_map(
        shards,
        mesh=mesh,
        in_specs=(P(("slab", "work"), None), P(("slab", "work")), P(), P(), P(), P(), P()),
        out_specs=P(("slab", "work"), None, None),
        check_vma=False,
    )
```

time: 216 us -> 51.2 us (0.24)
  the two profiles are of different devices: /device:TPU:1 before, /device:TPU:101 now
where the time goes in v1:
time: 51.2 us; the launch traced here: 50.8 us
  Pallas kernels  30.7 us (60%)
  local copies, waits for them, and re-layouts  7.98 us (16%)
  starting transfers between devices  7.23 us (14%)
  waiting for transfers between devices  4.85 us (9%)
    pallas_call x1, Pallas kernels, evaluate(): pl.pallas_call(unet, out_shape=(jax.ShapeDtypeStruct((OWNED, CLASSES, DEP...  28.9 us
    unnamed x20, local copies, waits for them, and re-layouts  6.12 us
    ppermute x1, starting transfers between devices, shards(): below = lax.ppermute(high, 'slab', up)  5.31 us
    ppermute x1, waiting for transfers between devices, shards(): above = lax.ppermute(low, 'slab', down)  4.84 us
    ppermute x1, starting transfers between devices, shards(): above = lax.ppermute(low, 'slab', down)  1.92 us
    pallas_call x1, local copies, waits for them, and re-layouts, shards(): pl.pallas_call(border_sum, out_shape=jax.ShapeDtypeStruct(core.shape, bf1...  1.86 us
    pallas_call x1, Pallas kernels, shards(): pl.pallas_call(border_sum, out_shape=jax.ShapeDtypeStruct(core.shape, bf1...  1.78 us
  transfers between devices with their start and end apart: 2, of which 1 were waited for; matrix products, arithmetic and copies ran while one was open for 0% of the time, Pallas kernels for 0%

profile of v1, /device:TPU:101, one launch (start us, length us, event | category | flops | bytes accessed | tf_op | source)
XLA Modules:
  0.0 50.8 jit_solution(14162483408633181083)
XLA Ops:
  0.0 0.0 copy-start.6
  0.0 0.0 copy-start.7
  0.0 0.7 %copy-done.6 = bf16[3,24]{1,0:T(4,128)(2,1)S(1)} copy-done((bf16[3,24]{1,0:T(4,128)(2,1)S(1)}, bf16[3,24]{1,0:T(4,128)(2,1)}, u32[]{:S(2)}) %copy-start.6) | copy-done | bytes 168
  0.7 0.0 copy-done.7
  0.7 0.0 copy-start.1
  0.7 0.9 %copy-done.1 = bf16[24,24,3,3,3]{1,0,4,3,2:T(8,128)(2,1)S(1)} copy-done((bf16[24,24,3,3,3]{1,0,4,3,2:T(8,128)(2,1)S(1)}, bf16[24,24,3,3,3]{1,0,4,3,2:T(8,128)(2,1)}, u32[]{:S(2)}) %copy-start.1) | copy-done | bytes 31128
  1.6 0.0 copy-start.2
  1.6 0.9 %copy-done.2 = bf16[48,24,3,3,3]{0,1,4,3,2:T(8,128)(2,1)S(1)} copy-done((bf16[48,24,3,3,3]{0,1,4,3,2:T(8,128)(2,1)S(1)}, bf16[48,24,3,3,3]{0,1,4,3,2:T(8,128)(2,1)}, u32[]{:S(2)}) %copy-start.2) | copy-done | bytes 62232
  2.5 0.9 %copy-done.3 = bf16[2,24576]{1,0:T(2,128)(2,1)S(1)} copy-done((bf16[2,24576]{1,0:T(2,128)(2,1)S(1)}, bf16[2,24576]{1,0:T(2,128)(2,1)}, u32[]{:S(2)}) %copy-start.3) | copy-done | bytes 98328
  3.4 0.0 copy-start.4
  3.4 0.7 %copy-done.4 = bf16[24,1,3,3,3]{0,4,3,2,1:T(4,128)(2,1)S(1)} copy-done((bf16[24,1,3,3,3]{0,4,3,2,1:T(4,128)(2,1)S(1)}, bf16[24,1,3,3,3]{0,4,3,2,1:T(4,128)(2,1)}, u32[]{:S(2)}) %copy-start.4) | copy-done | bytes 1320
  4.1 0.7 %copy-done.5 = bf16[24,48]{1,0:T(8,128)(2,1)S(1)} copy-done((bf16[24,48]{1,0:T(8,128)(2,1)S(1)}, bf16[24,48]{1,0:T(8,128)(2,1)}, u32[]{:S(2)}) %copy-start.5) | copy-done | bytes 2328
  4.8 28.9 %shard_map.73 = (bf16[2,3,16384]{2,1,0:T(4,128)(2,1)S(1)}, bf16[2,3,4096]{2,1,0:T(4,128)(2,1)S(1)}, bf16[2,3,4096]{2,1,0:T(4,128)(2,1)S(1)}) custom-call(s32[2]{0:T(128)S(1)} %copy-done.7, bf16[2,24576]{1,0:T(2,128)(2,1)S(1)} %copy-done.3, bf16[9,3,24]{2,1,0:T(4,128)(2,1)S(1)} %bitcast.11, bf16[27,24,24]{2,1,0:T(8,128)(2,1)S(1)} %bitcast.9, ...), custom_call_target="tpu_custom_call" | custom-call | tf_op jit(solution)/shard_map/pallas_call | solution.py:239
  33.7 0.0 copy-start
  33.7 0.7 %copy-done = bf16[2,3,16384]{2,1,0:T(4,128)(2,1)} copy-done((bf16[2,3,16384]{2,1,0:T(4,128)(2,1)}, bf16[2,3,16384]{2,1,0:T(4,128)(2,1)S(1)}, u32[]{:S(2)}) %copy-start) | copy-done | bytes 196632
  34.4 5.3 %collective-permute-start = (bf16[2,3,4096]{2,1,0:T(4,128)(2,1)S(1)}, bf16[2,3,4096]{2,1,0:T(4,128)(2,1)S(1)}, u32[]{:S(2)}, u32[]{:S(2)}) collective-permute-start(bf16[2,3,4096]{2,1,0:T(4,128)(2,1)S(1)} %get-tuple-element.9), channel_id=1, source_target_pairs={{0,16},{16,32},{32,48},{48,64},{64,80},{80,96},{96,112},{112,128},... | collective-permute-start | bytes 147464 | tf_op jit(solution)/shard_map/ppermute | solution.py:268
  39.7 1.9 %collective-permute-start.1 = (bf16[2,3,4096]{2,1,0:T(4,128)(2,1)S(1)}, bf16[2,3,4096]{2,1,0:T(4,128)(2,1)S(1)}, u32[]{:S(2)}, u32[]{:S(2)}) collective-permute-start(bf16[2,3,4096]{2,1,0:T(4,128)(2,1)S(1)} %get-tuple-element.10), channel_id=1, source_target_pairs={{16,0},{32,16},{48,32},{64,48},{80,64},{96,80},{112,96},{128,112},... | collective-permute-start | bytes 147464 | tf_op jit(solution)/shard_map/ppermute | solution.py:269
  41.7 0.0 collective-permute-done.below
  41.7 0.0 copy-start.8
  41.7 4.8 %collective-permute-done.1.above = bf16[2,3,4096]{2,1,0:T(4,128)(2,1)S(1)} collective-permute-done((bf16[2,3,4096]{2,1,0:T(4,128)(2,1)S(1)}, bf16[2,3,4096]{2,1,0:T(4,128)(2,1)S(1)}, u32[]{:S(2)}, u32[]{:S(2)}) %collective-permute-start.1) | collective-permute-done | bytes 49184 | tf_op jit(solution)/shard_map/ppermute | solution.py:269
  46.5 0.0 copy-done.8
  46.5 0.6 %copy-done.9 = bf16[2,3,4096]{2,1,0:T(4,128)(2,1)} copy-done((bf16[2,3,4096]{2,1,0:T(4,128)(2,1)}, bf16[2,3,4096]{2,1,0:T(4,128)(2,1)S(1)}, u32[]{:S(2)}) %copy-start.9) | copy-done | bytes 49176
  47.2 1.8 %shard_map.74 = bf16[2,3,16384]{2,1,0:T(4,128)(2,1)} custom-call(bf16[2,3,16384]{2,1,0:T(4,128)(2,1)} %copy-done, bf16[2,3,4096]{2,1,0:T(4,128)(2,1)} %copy-done.8, bf16[2,3,4096]{2,1,0:T(4,128)(2,1)} %copy-done.9), custom_call_target="tpu_custom_call" | custom-call | tf_op jit(solution)/shard_map/pallas_call | solution.py:270
  48.9 1.9 %copy.8 = bf16[2,3,16384]{2,0,1:T(2,128)(2,1)} copy(bf16[2,3,16384]{2,1,0:T(4,128)(2,1)} %shard_map.74) | data formatting | bytes 393216 | tf_op jit(solution)/shard_map/pallas_call | solution.py:270
  (3 shorter events, 0.0 us)
Async XLA Ops:
  0.0 0.7 %copy-start.6 = (bf16[3,24]{1,0:T(4,128)(2,1)S(1)}, bf16[3,24]{1,0:T(4,128)(2,1)}, u32[]{:S(2)}) copy-start(bf16[3,24]{1,0:T(4,128)(2,1)} %wout.1) | copy-start | bytes 436
  0.0 0.7 %copy-start.7 = (s32[2]{0:T(128)S(1)}, s32[2]{0:T(128)}, u32[]{:S(2)}) copy-start(s32[2]{0:T(128)} %tissue.1) | copy-start | bytes 28
  0.7 0.9 %copy-start.1 = (bf16[24,24,3,3,3]{1,0,4,3,2:T(8,128)(2,1)S(1)}, bf16[24,24,3,3,3]{1,0,4,3,2:T(8,128)(2,1)}, u32[]{:S(2)}) copy-start(bf16[24,24,3,3,3]{1,0,4,3,2:T(8,128)(2,1)} %param.10) | copy-start | bytes 93316
  1.6 0.9 %copy-start.2 = (bf16[48,24,3,3,3]{0,1,4,3,2:T(8,128)(2,1)S(1)}, bf16[48,24,3,3,3]{0,1,4,3,2:T(8,128)(2,1)}, u32[]{:S(2)}) copy-start(bf16[48,24,3,3,3]{0,1,4,3,2:T(8,128)(2,1)} %param.11) | copy-start | bytes 186628
  2.5 0.9 %copy-start.3 = (bf16[2,24576]{1,0:T(2,128)(2,1)S(1)}, bf16[2,24576]{1,0:T(2,128)(2,1)}, u32[]{:S(2)}) copy-start(bf16[2,24576]{1,0:T(2,128)(2,1)} %vol.1) | copy-start | bytes 294916
  3.4 0.7 %copy-start.4 = (bf16[24,1,3,3,3]{0,4,3,2,1:T(4,128)(2,1)S(1)}, bf16[24,1,3,3,3]{0,4,3,2,1:T(4,128)(2,1)}, u32[]{:S(2)}) copy-start(bf16[24,1,3,3,3]{0,4,3,2,1:T(4,128)(2,1)} %param.9) | copy-start | bytes 3892
  4.1 0.7 %copy-start.5 = (bf16[24,48]{1,0:T(8,128)(2,1)S(1)}, bf16[24,48]{1,0:T(8,128)(2,1)}, u32[]{:S(2)}) copy-start(bf16[24,48]{1,0:T(8,128)(2,1)} %wup.1) | copy-start | bytes 6916
  33.7 0.7 %copy-start = (bf16[2,3,16384]{2,1,0:T(4,128)(2,1)}, bf16[2,3,16384]{2,1,0:T(4,128)(2,1)S(1)}, u32[]{:S(2)}) copy-start(bf16[2,3,16384]{2,1,0:T(4,128)(2,1)S(1)} %get-tuple-element.8.core) | copy-start | bytes 589828
  34.4 7.2 %collective-permute-start = (bf16[2,3,4096]{2,1,0:T(4,128)(2,1)S(1)}, bf16[2,3,4096]{2,1,0:T(4,128)(2,1)S(1)}, u32[]{:S(2)}, u32[]{:S(2)}) collective-permute-start(bf16[2,3,4096]{2,1,0:T(4,128)(2,1)S(1)} %get-tuple-element.9), channel_id=1, source_target_pairs={{0,16},{16,32},{32,48},{48,64},{64,80},{80,96},{96,112},{112,128},... | collective-permute-start | bytes 147464 | tf_op jit(solution)/shard_map/ppermute | solution.py:268
  39.7 6.8 %collective-permute-start.1 = (bf16[2,3,4096]{2,1,0:T(4,128)(2,1)S(1)}, bf16[2,3,4096]{2,1,0:T(4,128)(2,1)S(1)}, u32[]{:S(2)}, u32[]{:S(2)}) collective-permute-start(bf16[2,3,4096]{2,1,0:T(4,128)(2,1)S(1)} %get-tuple-element.10), channel_id=1, source_target_pairs={{16,0},{32,16},{48,32},{64,48},{80,64},{96,80},{112,96},{128,112},... | collective-permute-start | bytes 147464 | tf_op jit(solution)/shard_map/ppermute | solution.py:269
  41.7 4.9 %copy-start.8 = (bf16[2,3,4096]{2,1,0:T(4,128)(2,1)}, bf16[2,3,4096]{2,1,0:T(4,128)(2,1)S(1)}, u32[]{:S(2)}) copy-start(bf16[2,3,4096]{2,1,0:T(4,128)(2,1)S(1)} %collective-permute-done.below) | copy-start | bytes 147460
  46.5 0.6 %copy-start.9 = (bf16[2,3,4096]{2,1,0:T(4,128)(2,1)}, bf16[2,3,4096]{2,1,0:T(4,128)(2,1)S(1)}, u32[]{:S(2)}) copy-start(bf16[2,3,4096]{2,1,0:T(4,128)(2,1)S(1)} %collective-permute-done.1.above) | copy-start | bytes 147460

commit v2 on v1

v2 whole, which is shorter than its diff:
```python
import functools

import jax
import jax.numpy as jnp
from jax import lax
from jax.experimental import pallas as pl
from jax.experimental.pallas import tpu as pltpu
from jax.sharding import PartitionSpec as P

SIDE = 32
DEPTH = 16
MARGIN = 4
EXTENT = 24
CHANNELS = 24
COARSE = 48
CLASSES = 3
OWNED = 2
HALF = EXTENT // 2
LANES = 256
PLANE = SIDE * SIDE
VROWS = 32
HROWS = 8 * CHANNELS
PROWS = 224
BIG = -1e30
UNROLL = 1

f32 = jnp.float32
bf16 = jnp.bfloat16


def dot(a, b):
    return jnp.dot(a, b, preferred_element_type=f32)


def iota(shape, dim):
    return lax.broadcasted_iota(jnp.int32, shape, dim)


def along_x(x, sx, xx):
    x = [pltpu.roll(x[:, 128 * d : 128 * d + 128], (-sx) % 128, 1) for d in range(2)]
    return jnp.where(xx == (15 if sx > 0 else 0), 0.0, jnp.concatenate(x, axis=1))


def along_y(x, sy, yy):
    x = [pltpu.roll(x[:, 128 * d : 128 * d + 128], (-16 * sy) % 128, 1) for d in range(2)]
    zero = jnp.zeros_like(x[0])
    edge = yy[:, 0:128] == (7 if sy > 0 else 0)
    low = jnp.where(edge, x[1] if sy > 0 else zero, x[0])
    high = jnp.where(edge, zero if sy > 0 else x[0], x[1])
    return jnp.concatenate([low, high], axis=1)


def shifted(x, sy, sx, yy, xx):
    x = along_x(x, sx, xx) if sx else x
    return along_y(x, sy, yy) if sy else x


def swap_chunks(parts, low):
    out = []
    for j in range(4):
        halves = []
        for d in range(2):
            piece = [parts[2 * d + i][:, 128 * (j // 2) : 128 * (j // 2) + 128] for i in range(2)]
            if j % 2 == 0:
                halves.append(jnp.where(low, piece[0], pltpu.roll(piece[1], 64, 1)))
            else:
                halves.append(jnp.where(low, pltpu.roll(piece[0], 64, 1), piece[1]))
        out.append(jnp.concatenate(halves, axis=1))
    return out


def unet(*refs):
    hbm, (core, low_out, high_out), local = refs[:7], refs[7:10], refs[10:17]
    sems = refs[17]
    copies = [pltpu.make_async_copy(a, c, sems.at[k]) for k, (a, c) in enumerate(zip(hbm, local))]
    for copy in copies:
        copy.start()
    evaluate_bricks(copies, *local, core, low_out, high_out, *refs[18:])


def evaluate_bricks(
    copies, tissue, vol, w1, w2, wd, wup, wout, core, low_out, high_out,
    t1, b2, td, w1big, w2big, wd3, wo, vs, vz, hx, fs, ps, px, ys, gs, us, zs, rs,
):
    lane = iota((1, LANES), 1)
    yy, xx = lane >> 4, lane & 15
    low64 = iota((1, 128), 1) < 64

    for b in range(OWNED):
        vz[b] = jnp.zeros((2, 26 * VROWS, 128), f32)
        hx[b, 0:HROWS] = jnp.zeros((HROWS, LANES), bf16)
        hx[b, 25 * HROWS : 26 * HROWS] = jnp.zeros((HROWS, LANES), bf16)
        ys[b, 0] = jnp.zeros((144, LANES), f32)
        ys[b, HALF + 1] = jnp.zeros((144, LANES), f32)
        for row, m in ((24, yy == 0), (25, yy == 15)):
            for d in range(2):
                vz[b, d, pl.ds(row, 26, stride=VROWS), :] = jnp.broadcast_to(
                    m[:, 128 * d : 128 * d + 128].astype(f32), (26, 128)
                )
    t1[...] = jnp.zeros_like(t1)
    b2[...] = jnp.zeros_like(b2)
    td[...] = jnp.zeros_like(td)
    for copy in copies:
        copy.wait()

    for kz in range(3):
        for ky in range(3):
            at = kz * VROWS + ky * 4
            t1[at : at + 3, 0:CHANNELS] = w1[kz * 3 + ky].astype(f32)
    base1 = t1[...].T[0:CHANNELS]
    for pz in range(2):
        for ey in range(4):
            rows = []
            for ox in range(2):
                s = pz * VROWS + ey * 4 + ox
                m = pltpu.roll(base1, s, 1) if s else base1
                if ey in (0, 3):
                    m = jnp.where(lane[:, 0:128] == (24 if ey == 0 else 25), BIG, m)
                rows.append(m)
            at = (pz * 8 + ey * 2) * CHANNELS
            w1big[at : at + 48] = jnp.concatenate(rows, axis=0).astype(bf16)

    for ox in range(4):
        for kz in range(3):
            for ky in range(3):
                piece = [
                    w2[kz * 9 + ky * 3 + 2 - ox + dx].astype(f32)
                    if 0 <= 2 - ox + dx < 3
                    else jnp.zeros((CHANNELS, CHANNELS), f32)
                    for dx in range(2)
                ]
                at = kz * HROWS + ky * 48
                b2[ox, :, at : at + 48] = jnp.concatenate(piece, axis=1)
    for ox in range(4):
        base2 = b2[ox]
        for oz in range(2):
            rows = []
            for oy in range(2):
                s = oz * HROWS + oy * 48
                rows.append(pltpu.roll(base2, s, 1) if s else base2)
            at = (ox * 4 + oz * 2) * CHANNELS
            w2big[at : at + 48] = jnp.concatenate(rows, axis=0).astype(bf16)

    for kz in range(3):
        for k in range(9):
            td[kz, k * 24 : k * 24 + 24, 0:COARSE] = wd[kz * 9 + k].astype(f32)
    for kz in range(3):
        wd3[kz * COARSE : kz * COARSE + COARSE] = td[kz].T[0:COARSE, 0:PROWS].astype(bf16)

    ci = iota((CHANNELS, 192), 0)
    col = iota((CHANNELS, 192), 1)
    tiled = dot(wout[...], (col % 24 == ci).astype(bf16))
    r = iota((32, 192), 0)
    c = iota((32, 192), 1) // 24
    acc = jnp.zeros((32, 192), f32)
    for cls in range(CLASSES):
        acc = acc + jnp.where((r & 3) == cls, tiled[cls : cls + 1], 0.0)
    cell = ((r >> 3) & 1) * 4 + ((r >> 2) & 1) * 2 + (r >> 4)
    wo[...] = jnp.where(c == cell, acc, 0.0).astype(bf16)

    def source(l):
        p = l >> 6
        return ((l >> 4) & 3) * 64 + (p >> 1) * 32 + (l & 15) * 2 + (p & 1)

    sort = (iota((LANES, LANES), 0) == source(lane)).astype(bf16)
    unsort = (iota((LANES, LANES), 1) == source(iota((LANES, 1), 0))).astype(bf16)

    for z in range(EXTENT):
        for t in range(4):
            at = z * PLANE + t * LANES
            for d in range(2):
                vs[d, pl.ds(t * EXTENT + z, OWNED, stride=96), :] = vol[
                    :, at + 128 * d : at + 128 * d + 128
                ].astype(f32)
    sorted_cells = dot(jnp.concatenate([vs[0], vs[1]], axis=1).astype(bf16), sort)
    for b in range(OWNED):
        parts = [sorted_cells[b * 96 + t * 24 : b * 96 + t * 24 + 24] for t in range(4)]
        parities = swap_chunks(parts, low64)
        for p in range(4):
            for sy in (-1, 0, 1):
                for sx in ((0, 1) if p & 1 == 0 else (-1, 0)):
                    row = (2 * sy + (p >> 1) + 2) * 4 + 2 * sx + (p & 1) + 1
                    near = shifted(parities[p], sy, sx, yy, xx)
                    for d in range(2):
                        vz[b, d, pl.ds(VROWS + row, EXTENT, stride=VROWS), :] = near[
                            :, 128 * d : 128 * d + 128
                        ]

    def first(j):
        b, i = j // HALF, j % HALF
        at = i * (2 * VROWS)
        if not isinstance(j, int):
            at = pl.multiple_of(at, 2 * VROWS)
        near = [vz[b, d, pl.ds(at, 4 * VROWS), :] for d in range(2)]
        near = jnp.concatenate(near, axis=1).astype(bf16)
        out = jnp.maximum(dot(w1big[...], near), 0.0).astype(bf16)
        to = i * (2 * HROWS) + HROWS
        if not isinstance(j, int):
            to = pl.multiple_of(to, HROWS)
        hx[b, pl.ds(to, 2 * HROWS), :] = out

    def second(j):
        b, i = j // HALF, j % HALF
        at = i * (2 * HROWS)
        if not isinstance(j, int):
            at = pl.multiple_of(at, 2 * HROWS)
        out = dot(w2big[...], hx[b, pl.ds(at, 4 * HROWS), :])
        left = out[96:192] + along_x(out[288:384], -1, xx)
        right = out[192:288] + along_x(out[0:96], 1, xx)
        fine = jnp.maximum(jnp.concatenate([left, right], axis=0), 0.0)
        fs[b, i] = fine.astype(bf16)
        ps[j] = functools.reduce(jnp.maximum, [fine[c * 24 : c * 24 + 24] for c in range(8)])

    def spread(j):
        p = ps[j]
        near = [shifted(p, sy, sx, yy, xx) for sy in (-1, 0, 1) for sx in (-1, 0, 1)]
        near = jnp.concatenate(near + [jnp.zeros((8, LANES), f32)], axis=0).astype(bf16)
        px[j] = near

    def coarse(j):
        b, i = j // HALF, j % HALF
        ys[b, i + 1] = dot(wd3[...], px[j])

    def gather(j):
        b, i = j // HALF, j % HALF
        g = ys[b, i, 0:48] + ys[b, i + 1, 48:96] + ys[b, i + 2, 96:144]
        gs[j] = jnp.maximum(g, 0.0).astype(bf16)

    def lift(j):
        us[j] = dot(wup[...], gs[j])

    def mix(j):
        b, i = j // HALF, j % HALF
        fine = fs[b, i].astype(f32).reshape(8, CHANNELS, LANES)
        z = jnp.maximum(fine + us[j][None], 0.0).reshape(8 * CHANNELS, LANES)
        zs[j] = z.astype(bf16)

    def project(j):
        b, i = j // HALF, j % HALF
        pred = jax.nn.sigmoid(dot(wo[...], zs[j]))
        pred = jnp.where(tissue[b] == 1, pred, 0.0)
        for p in range(4):
            for d in range(2):
                rs[p, d, pl.ds(i * 16 + b, 8, stride=2), :] = pred[
                    p * 8 : p * 8 + 8, 128 * d : 128 * d + 128
                ]

    units = OWNED * HALF

    stages = ((second, 0), (first, 2), (coarse, -2), (lift, -5), (project, -7), (spread, -1), (gather, -4), (mix, -6))
    for j in range(-2, units + 7):
        for stage, lag in stages:
            if 0 <= j + lag < units:
                stage(j + lag)

    chunks = swap_chunks([jnp.concatenate([rs[p, 0], rs[p, 1]], axis=1) for p in range(4)], low64)
    for t in range(4):
        rows = dot(chunks[t].astype(bf16), unsort)
        for z in range(EXTENT):
            if z < MARGIN:
                to, ref = z, low_out
            elif z < MARGIN + DEPTH:
                to, ref = z - MARGIN, core
            else:
                to, ref = z - MARGIN - DEPTH, high_out
            for cls in range(CLASSES):
                piece = rows[z * 8 + cls * 2 : z * 8 + cls * 2 + 2].astype(bf16)
                ref[cls, :, to * PLANE + t * LANES : to * PLANE + t * LANES + LANES] = piece


VMEM = pl.BlockSpec(memory_space=pltpu.VMEM)


def evaluate(volume, tissue, w_first, w_second, w_down, w_up, w_out):
    w1 = jnp.transpose(w_first, (1, 2, 3, 4, 0)).reshape(9, 3, CHANNELS)
    w2 = jnp.transpose(w_second, (2, 3, 4, 0, 1)).reshape(27, CHANNELS, CHANNELS)
    wd = jnp.transpose(w_down, (2, 3, 4, 1, 0)).reshape(27, CHANNELS, COARSE)
    edge = jax.ShapeDtypeStruct((CLASSES, OWNED, MARGIN * PLANE), bf16)
    arrays = [pltpu.with_memory_space_constraint(a, pltpu.HBM) for a in (tissue, volume, w1, w2, wd, w_up, w_out)]
    return pl.pallas_call(
        unet,
        out_shape=(jax.ShapeDtypeStruct((CLASSES, OWNED, DEPTH * PLANE), bf16), edge, edge),
        in_specs=[pl.BlockSpec(memory_space=pltpu.HBM)] * 7,
        out_specs=(VMEM,) * 3,
        scratch_shapes=[pltpu.SMEM(tissue.shape, tissue.dtype)]
        + [pltpu.VMEM(a.shape, a.dtype) for a in arrays[1:]]
        + [
            pltpu.SemaphoreType.DMA((7,)),
            pltpu.VMEM((128, 128), f32),
            pltpu.VMEM((4, CHANNELS, 4 * HROWS), f32),
            pltpu.VMEM((3, 256, 128), f32),
            pltpu.VMEM((2 * HROWS, 4 * VROWS), bf16),
            pltpu.VMEM((384, 4 * HROWS), bf16),
            pltpu.VMEM((144, PROWS), bf16),
            pltpu.VMEM((32, 192), bf16),
            pltpu.VMEM((2, 192, 128), f32),
            pltpu.VMEM((OWNED, 2, 26 * VROWS, 128), f32),
            pltpu.VMEM((OWNED, 26 * HROWS, LANES), bf16),
            pltpu.VMEM((OWNED, HALF, 192, LANES), bf16),
            pltpu.VMEM((OWNED * HALF, CHANNELS, LANES), f32),
            pltpu.VMEM((OWNED * HALF, PROWS, LANES), bf16),
            pltpu.VMEM((OWNED, HALF + 2, 144, LANES), f32),
            pltpu.VMEM((OWNED * HALF, COARSE, LANES), bf16),
            pltpu.VMEM((OWNED * HALF, CHANNELS, LANES), f32),
            pltpu.VMEM((OWNED * HALF, 8 * CHANNELS, LANES), bf16),
            pltpu.VMEM((4, 2, EXTENT * 8, 128), f32),
        ],
        compiler_params=pltpu.CompilerParams(vmem_limit_bytes=48 << 20),
    )(*arrays)


def shards(volume, tissue, w_first, w_second, w_down, w_up, w_out):
    core, low, high = evaluate(volume, tissue, w_first, w_second, w_down, w_up, w_out)
    slabs = lax.axis_size("slab")
    up = [(i, i + 1) for i in range(slabs - 1)]
    down = [(i + 1, i) for i in range(slabs - 1)]
    below = lax.ppermute(high, "slab", up)
    above = lax.ppermute(low, "slab", down)
    rest = DEPTH * PLANE - MARGIN * PLANE
    total = core.astype(f32)
    total = total + jnp.pad(below.astype(f32), ((0, 0), (0, 0), (0, rest)))
    total = total + jnp.pad(above.astype(f32), ((0, 0), (0, 0), (rest, 0)))
    return jnp.transpose(total.astype(bf16), (1, 0, 2))


def solution(mesh):
    return jax.shard_map(
        shards,
        mesh=mesh,
        in_specs=(P(("slab", "work"), None), P(("slab", "work")), P(), P(), P(), P(), P()),
        out_specs=P(("slab", "work"), None, None),
        check_vma=False,
    )
```

time: 51.2 us -> 23.2 us (0.45)
  the two profiles are of different devices: /device:TPU:101 before, /device:TPU:253 now
where the time goes in v2:
time: 23.2 us; the launch traced here: 23 us
  Pallas kernels  10.2 us (44%)
  starting transfers between devices  7.26 us (31%)
  waiting for transfers between devices  4.68 us (20%)
  other arithmetic  0.88 us (4%)
    pallas_call x1, Pallas kernels, evaluate(): pl.pallas_call(unet, out_shape=(jax.ShapeDtypeStruct((CLASSES, OWNED, DEP...  10.2 us
    ppermute x1, starting transfers between devices, shards(): below = lax.ppermute(high, 'slab', up)  5.34 us
    ppermute x1, waiting for transfers between devices, shards(): above = lax.ppermute(low, 'slab', down)  4.68 us
    ppermute x1, starting transfers between devices, shards(): above = lax.ppermute(low, 'slab', down)  1.92 us
    transpose x1, other arithmetic, shards(): return jnp.transpose(total.astype(bf16), (1, 0, 2))  0.88 us
  transfers between devices with their start and end apart: 2, of which 1 were waited for; matrix products, arithmetic and copies ran while one was open for 0% of the time, Pallas kernels for 0%

profile of v2, /device:TPU:253, one launch (start us, length us, event | category | flops | bytes accessed | tf_op | source)
XLA Modules:
  0.0 23.0 jit_solution(11888465189232573554)
XLA Ops:
  0.0 10.2 %shard_map.73 = (bf16[3,2,16384]{2,1,0:T(2,128)(2,1)S(1)}, bf16[3,2,4096]{2,1,0:T(2,128)(2,1)S(1)}, bf16[3,2,4096]{2,1,0:T(2,128)(2,1)S(1)}) custom-call(s32[2]{0:T(128)} %refs_0_.1, bf16[2,24576]{1,0:T(2,128)(2,1)} %refs_1_.1, bf16[9,3,24]{2,1,0:T(4,128)(2,1)} %bitcast.13, bf16[27,24,24]{2,1,0:T(8,128)(2,1)} %bitcast.11, bf16[27,24,48]{2,1,0:T(8,128)(2,1)} %bitcast.12, ...), custom_call_target="tpu_custom_call" | custom-call | tf_op jit(solution)/shard_map/pallas_call | solution.py:280
  10.2 5.3 %collective-permute-start = (bf16[3,2,4096]{2,1,0:T(2,128)(2,1)S(1)}, bf16[3,2,4096]{2,1,0:T(2,128)(2,1)S(1)}, u32[]{:S(2)}, u32[]{:S(2)}) collective-permute-start(bf16[3,2,4096]{2,1,0:T(2,128)(2,1)S(1)} %get-tuple-element.9), channel_id=1, source_target_pairs={{0,16},{16,32},{32,48},{48,64},{64,80},{80,96},{96,112},{112,128},... | collective-permute-start | bytes 147464 | tf_op jit(solution)/shard_map/ppermute | solution.py:317
  15.6 1.9 %collective-permute-start.1 = (bf16[3,2,4096]{2,1,0:T(2,128)(2,1)S(1)}, bf16[3,2,4096]{2,1,0:T(2,128)(2,1)S(1)}, u32[]{:S(2)}, u32[]{:S(2)}) collective-permute-start(bf16[3,2,4096]{2,1,0:T(2,128)(2,1)S(1)} %get-tuple-element.10), channel_id=1, source_target_pairs={{16,0},{32,16},{48,32},{64,48},{80,64},{96,80},{112,96},{128,112},... | collective-permute-start | bytes 147464 | tf_op jit(solution)/shard_map/ppermute | solution.py:318
  17.5 0.0 collective-permute-done
  17.5 4.7 %collective-permute-done.1 = bf16[3,2,4096]{2,1,0:T(2,128)(2,1)S(1)} collective-permute-done((bf16[3,2,4096]{2,1,0:T(2,128)(2,1)S(1)}, bf16[3,2,4096]{2,1,0:T(2,128)(2,1)S(1)}, u32[]{:S(2)}, u32[]{:S(2)}) %collective-permute-start.1) | collective-permute-done | bytes 49184 | tf_op jit(solution)/shard_map/ppermute | solution.py:318
  22.2 0.9 %fusion = bf16[2,3,16384]{2,0,1:T(2,128)(2,1)} fusion(bf16[3,2,16384]{2,1,0:T(2,128)(2,1)S(1)} %get-tuple-element.8, bf16[3,2,4096]{2,1,0:T(2,128)(2,1)S(1)} %collective-permute-done.1, bf16[3,2,4096]{2,1,0:T(2,128)(2,1)S(1)} %collective-permute-done), kind=kLoop, calls=%fused_computation.1 | loop fusion | flops 589824 | bytes 491520 | tf_op jit(solution)/shard_map/transpose | solution.py:323
Async XLA Ops:
  10.2 7.3 %collective-permute-start = (bf16[3,2,4096]{2,1,0:T(2,128)(2,1)S(1)}, bf16[3,2,4096]{2,1,0:T(2,128)(2,1)S(1)}, u32[]{:S(2)}, u32[]{:S(2)}) collective-permute-start(bf16[3,2,4096]{2,1,0:T(2,128)(2,1)S(1)} %get-tuple-element.9), channel_id=1, source_target_pairs={{0,16},{16,32},{32,48},{48,64},{64,80},{80,96},{96,112},{112,128},... | collective-permute-start | bytes 147464 | tf_op jit(solution)/shard_map/ppermute | solution.py:317
  15.6 6.6 %collective-permute-start.1 = (bf16[3,2,4096]{2,1,0:T(2,128)(2,1)S(1)}, bf16[3,2,4096]{2,1,0:T(2,128)(2,1)S(1)}, u32[]{:S(2)}, u32[]{:S(2)}) collective-permute-start(bf16[3,2,4096]{2,1,0:T(2,128)(2,1)S(1)} %get-tuple-element.10), channel_id=1, source_target_pairs={{16,0},{32,16},{48,32},{64,48},{80,64},{96,80},{112,96},{128,112},... | collective-permute-start | bytes 147464 | tf_op jit(solution)/shard_map/ppermute | solution.py:318

commit v3 on v2

--- a/solution.py
+++ b/solution.py
@@ -22,8 +22,7 @@
 HROWS = 8 * CHANNELS
 PROWS = 224
 BIG = -1e30
-UNROLL = 1
-
+NAMES = ("volume", "first", "second", "coarse", "up", "out", "tissue")
 f32 = jnp.float32
 bf16 = jnp.bfloat16
 
@@ -79,7 +78,7 @@
 
 
 def evaluate_bricks(
-    copies, tissue, vol, w1, w2, wd, wup, wout, core, low_out, high_out,
+    copies, vol, w1, w2, wd, wup, wout, tissue, core, low_out, high_out,
     t1, b2, td, w1big, w2big, wd3, wo, vs, vz, hx, fs, ps, px, ys, gs, us, zs, rs,
 ):
     lane = iota((1, LANES), 1)
@@ -100,8 +99,9 @@
     t1[...] = jnp.zeros_like(t1)
     b2[...] = jnp.zeros_like(b2)
     td[...] = jnp.zeros_like(td)
-    for copy in copies:
-        copy.wait()
+    wait = {name: copy.wait for name, copy in zip(NAMES, copies)}
+    wait["volume"]()
+    wait["first"]()
 
     for kz in range(3):
         for ky in range(3):
@@ -119,44 +119,6 @@
                 rows.append(m)
             at = (pz * 8 + ey * 2) * CHANNELS
             w1big[at : at + 48] = jnp.concatenate(rows, axis=0).astype(bf16)
-
-    for ox in range(4):
-        for kz in range(3):
-            for ky in range(3):
-                piece = [
-                    w2[kz * 9 + ky * 3 + 2 - ox + dx].astype(f32)
-                    if 0 <= 2 - ox + dx < 3
-                    else jnp.zeros((CHANNELS, CHANNELS), f32)
-                    for dx in range(2)
-                ]
-                at = kz * HROWS + ky * 48
-                b2[ox, :, at : at + 48] = jnp.concatenate(piece, axis=1)
-    for ox in range(4):
-        base2 = b2[ox]
-        for oz in range(2):
-            rows = []
-            for oy in range(2):
-                s = oz * HROWS + oy * 48
-                rows.append(pltpu.roll(base2, s, 1) if s else base2)
-            at = (ox * 4 + oz * 2) * CHANNELS
-            w2big[at : at + 48] = jnp.concatenate(rows, axis=0).astype(bf16)
-
-    for kz in range(3):
-        for k in range(9):
-            td[kz, k * 24 : k * 24 + 24, 0:COARSE] = wd[kz * 9 + k].astype(f32)
-    for kz in range(3):
-        wd3[kz * COARSE : kz * COARSE + COARSE] = td[kz].T[0:COARSE, 0:PROWS].astype(bf16)
-
-    ci = iota((CHANNELS, 192), 0)
-    col = iota((CHANNELS, 192), 1)
-    tiled = dot(wout[...], (col % 24 == ci).astype(bf16))
-    r = iota((32, 192), 0)
-    c = iota((32, 192), 1) // 24
-    acc = jnp.zeros((32, 192), f32)
-    for cls in range(CLASSES):
-        acc = acc + jnp.where((r & 3) == cls, tiled[cls : cls + 1], 0.0)
-    cell = ((r >> 3) & 1) * 4 + ((r >> 2) & 1) * 2 + (r >> 4)
-    wo[...] = jnp.where(c == cell, acc, 0.0).astype(bf16)
 
     def source(l):
         p = l >> 6
@@ -186,24 +148,64 @@
                             :, 128 * d : 128 * d + 128
                         ]
 
+    def second_weights():
+        wait["second"]()
+        for ox in range(4):
+            for kz in range(3):
+                for ky in range(3):
+                    piece = [
+                        w2[kz * 9 + ky * 3 + 2 - ox + dx].astype(f32)
+                        if 0 <= 2 - ox + dx < 3
+                        else jnp.zeros((CHANNELS, CHANNELS), f32)
+                        for dx in range(2)
+                    ]
+                    at = kz * HROWS + ky * 48
+                    b2[ox, :, at : at + 48] = jnp.concatenate(piece, axis=1)
+        for ox in range(4):
+            base2 = b2[ox]
+            for oz in range(2):
+                rows = []
+                for oy in range(2):
+                    s = oz * HROWS + oy * 48
+                    rows.append(pltpu.roll(base2, s, 1) if s else base2)
+                at = (ox * 4 + oz * 2) * CHANNELS
+                w2big[at : at + 48] = jnp.concatenate(rows, axis=0).astype(bf16)
+
+    def coarse_weights():
+        wait["coarse"]()
+        for kz in range(3):
+            for k in range(9):
+                td[kz, k * 24 : k * 24 + 24, 0:COARSE] = wd[kz * 9 + k].astype(f32)
+        for kz in range(3):
+            wd3[kz * COARSE : kz * COARSE + COARSE] = td[kz].T[0:COARSE, 0:PROWS].astype(bf16)
+
+    def out_weights():
+        wait["up"]()
+        wait["out"]()
+        wait["tissue"]()
+        ci = iota((CHANNELS, 192), 0)
+        col = iota((CHANNELS, 192), 1)
+        tiled = dot(wout[...], (col % 24 == ci).astype(bf16))
+        r = iota((32, 192), 0)
+        c = iota((32, 192), 1) // 24
+        acc = jnp.zeros((32, 192), f32)
+        for cls in range(CLASSES):
+            acc = acc + jnp.where((r & 3) == cls, tiled[cls : cls + 1], 0.0)
+        cell = ((r >> 3) & 1) * 4 + ((r >> 2) & 1) * 2 + (r >> 4)
+        wo[...] = jnp.where(c == cell, acc, 0.0).astype(bf16)
+
     def first(j):
         b, i = j // HALF, j % HALF
         at = i * (2 * VROWS)
-        if not isinstance(j, int):
-            at = pl.multiple_of(at, 2 * VROWS)
         near = [vz[b, d, pl.ds(at, 4 * VROWS), :] for d in range(2)]
         near = jnp.concatenate(near, axis=1).astype(bf16)
         out = jnp.maximum(dot(w1big[...], near), 0.0).astype(bf16)
         to = i * (2 * HROWS) + HROWS
-        if not isinstance(j, int):
-            to = pl.multiple_of(to, HROWS)
         hx[b, pl.ds(to, 2 * HROWS), :] = out
 
     def second(j):
         b, i = j // HALF, j % HALF
         at = i * (2 * HROWS)
-        if not isinstance(j, int):
-            at = pl.multiple_of(at, 2 * HROWS)
         out = dot(w2big[...], hx[b, pl.ds(at, 4 * HROWS), :])
         left = out[96:192] + along_x(out[288:384], -1, xx)
         right = out[192:288] + along_x(out[0:96], 1, xx)
@@ -245,27 +247,35 @@
                     p * 8 : p * 8 + 8, 128 * d : 128 * d + 128
                 ]
 
+    def emit():
+        parts = [jnp.concatenate([rs[p, d] for d in range(2)], axis=1) for p in range(4)]
+        chunks = swap_chunks(parts, low64)
+        for t in range(4):
+            rows = dot(chunks[t].astype(bf16), unsort)
+            for z in range(EXTENT):
+                if z < MARGIN:
+                    to, ref = z, low_out
+                elif z < MARGIN + DEPTH:
+                    to, ref = z - MARGIN, core
+                else:
+                    to, ref = z - MARGIN - DEPTH, high_out
+                to = to * PLANE + t * LANES
+                for cls in range(CLASSES):
+                    piece = rows[z * 8 + cls * 2 : z * 8 + cls * 2 + 2]
+                    ref[cls, :, to : to + LANES] = piece.astype(bf16)
+
     units = OWNED * HALF
-
-    stages = ((second, 0), (first, 2), (coarse, -2), (lift, -5), (project, -7), (spread, -1), (gather, -4), (mix, -6))
+    second_weights()
+    coarse_weights()
+    out_weights()
     for j in range(-2, units + 7):
-        for stage, lag in stages:
+        for stage, lag in (
+            (second, 0), (first, 2), (coarse, -2), (lift, -5),
+            (project, -7), (spread, -1), (gather, -4), (mix, -6),
+        ):
             if 0 <= j + lag < units:
                 stage(j + lag)
-
-    chunks = swap_chunks([jnp.concatenate([rs[p, 0], rs[p, 1]], axis=1) for p in range(4)], low64)
-    for t in range(4):
-        rows = dot(chunks[t].astype(bf16), unsort)
-        for z in range(EXTENT):
-            if z < MARGIN:
-                to, ref = z, low_out
-            elif z < MARGIN + DEPTH:
-                to, ref = z - MARGIN, core
-            else:
-                to, ref = z - MARGIN - DEPTH, high_out
-            for cls in range(CLASSES):
-                piece = rows[z * 8 + cls * 2 : z * 8 + cls * 2 + 2].astype(bf16)
-                ref[cls, :, to * PLANE + t * LANES : to * PLANE + t * LANES + LANES] = piece
+    emit()
 
 
 VMEM = pl.BlockSpec(memory_space=pltpu.VMEM)
@@ -276,15 +286,15 @@
     w2 = jnp.transpose(w_second, (2, 3, 4, 0, 1)).reshape(27, CHANNELS, CHANNELS)
     wd = jnp.transpose(w_down, (2, 3, 4, 1, 0)).reshape(27, CHANNELS, COARSE)
     edge = jax.ShapeDtypeStruct((CLASSES, OWNED, MARGIN * PLANE), bf16)
-    arrays = [pltpu.with_memory_space_constraint(a, pltpu.HBM) for a in (tissue, volume, w1, w2, wd, w_up, w_out)]
+    arrays = [pltpu.with_memory_space_constraint(a, pltpu.HBM) for a in (volume, w1, w2, wd, w_up, w_out, tissue)]
     return pl.pallas_call(
         unet,
         out_shape=(jax.ShapeDtypeStruct((CLASSES, OWNED, DEPTH * PLANE), bf16), edge, edge),
         in_specs=[pl.BlockSpec(memory_space=pltpu.HBM)] * 7,
         out_specs=(VMEM,) * 3,
-        scratch_shapes=[pltpu.SMEM(tissue.shape, tissue.dtype)]
-        + [pltpu.VMEM(a.shape, a.dtype) for a in arrays[1:]]
+        scratch_shapes=[pltpu.VMEM(a.shape, a.dtype) for a in arrays[:6]]
         + [
+            pltpu.SMEM(tissue.shape, tissue.dtype),
             pltpu.SemaphoreType.DMA((7,)),
             pltpu.VMEM((128, 128), f32),
             pltpu.VMEM((4, CHANNELS, 4 * HROWS), f32),
@@ -312,10 +322,15 @@
 def shards(volume, tissue, w_first, w_second, w_down, w_up, w_out):
     core, low, high = evaluate(volume, tissue, w_first, w_second, w_down, w_up, w_out)
     slabs = lax.axis_size("slab")
-    up = [(i, i + 1) for i in range(slabs - 1)]
-    down = [(i + 1, i) for i in range(slabs - 1)]
-    below = lax.ppermute(high, "slab", up)
-    above = lax.ppermute(low, "slab", down)
+    me = lax.axis_index("slab")
+    odd = (me % 2) == 1
+    across = [(i, i + 1) for i in range(1, slabs - 1, 2)] + [(i + 1, i) for i in range(1, slabs - 1, 2)]
+    chip = [[i, i + 1] for i in range(0, slabs, 2)]
+    two = lax.ppermute(jnp.where(odd, high, low), "slab", across)
+    one = lax.all_gather(jnp.where(odd, low, high), "slab", axis_index_groups=chip)
+    one = jnp.where(odd, one[0], one[1])
+    above = jnp.where(odd, two, one)
+    below = jnp.where(odd, one, two)
     rest = DEPTH * PLANE - MARGIN * PLANE
     total = core.astype(f32)
     total = total + jnp.pad(below.astype(f32), ((0, 0), (0, 0), (0, rest)))

time: 23.2 us -> 20.9 us (0.901)
  the two profiles are of different devices: /device:TPU:253 before, /device:TPU:1 now
where the time goes in v3:
time: 20.9 us; the launch traced here: 20.8 us
  Pallas kernels  10.7 us (51%)
  starting transfers between devices  4.92 us (24%)
  blocking collectives  4.14 us (20%)
  other arithmetic  1.06 us (5%)
    pallas_call x1, Pallas kernels, evaluate(): pl.pallas_call(unet, out_shape=(jax.ShapeDtypeStruct((CLASSES, OWNED, DEP...  10.7 us
    ppermute x1, starting transfers between devices, shards(): two = lax.ppermute(jnp.where(odd, high, low), 'slab', across)  4.92 us
    all_gather x1, blocking collectives, shards(): lax.all_gather(jnp.where(odd, low, high), 'slab', axis_index_groups=chip)  4.14 us
    transpose x1, other arithmetic, shards(): return jnp.transpose(total.astype(bf16), (1, 0, 2))  0.88 us
  transfers between devices with their start and end apart: 1, of which 0 were waited for; matrix products, arithmetic and copies ran while one was open for 0% of the time, Pallas kernels for 0%

profile of v3, /device:TPU:1, one launch (start us, length us, event | category | flops | bytes accessed | tf_op | source)
XLA Modules:
  0.0 20.8 jit_solution(17607079849294790193)
XLA Ops:
  0.0 10.7 %shard_map.73 = (bf16[3,2,16384]{2,1,0:T(2,128)(2,1)S(1)}, bf16[3,2,4096]{2,1,0:T(2,128)(2,1)S(1)}, bf16[3,2,4096]{2,1,0:T(2,128)(2,1)S(1)}) custom-call(bf16[2,24576]{1,0:T(2,128)(2,1)} %refs_0_.1, bf16[9,3,24]{2,1,0:T(4,128)(2,1)} %bitcast.13, bf16[27,24,24]{2,1,0:T(8,128)(2,1)} %bitcast.11, bf16[27,24,48]{2,1,0:T(8,128)(2,1)} %bitcast.12, ...), custom_call_target="tpu_custom_call" | custom-call | tf_op jit(solution)/shard_map/pallas_call | solution.py:290
  10.7 0.1 broadcast_select_fusion.4
  10.8 4.9 %collective-permute-start = (bf16[3,2,4096]{2,1,0:T(2,128)(2,1)S(1)}, bf16[3,2,4096]{2,1,0:T(2,128)(2,1)S(1)}, u32[]{:S(2)}, u32[]{:S(2)}) collective-permute-start(bf16[3,2,4096]{2,1,0:T(2,128)(2,1)S(1)} %get-tuple-element.14), channel_id=1, source_target_pairs={{16,32},{48,64},{80,96},{112,128},{144,160},{176,192},{208,224},{2... | collective-permute-start | bytes 147464 | tf_op jit(solution)/shard_map/ppermute | solution.py:329
  15.7 4.1 %all-gather = bf16[6,2,4096]{2,1,0:T(2,128)(2,1)S(1)} all-gather(bf16[3,2,4096]{2,1,0:T(2,128)(2,1)S(1)} %get-tuple-element.13), channel_id=2, replica_groups={{0,16},{32,48},{64,80},{96,112},{128,144},{160,176},{192,208},{224,240}..., dimensions={0}, use_global_device_ids=true | all-gather | bytes 147456 | tf_op jit(solution)/shard_map/all_gather | solution.py:330
  19.8 0.0 collective-permute-done
  19.8 0.1 broadcast_select_fusion.2
  19.9 0.9 %fusion = bf16[2,3,16384]{2,0,1:T(2,128)(2,1)} fusion(bf16[3,2,16384]{2,1,0:T(2,128)(2,1)S(1)} %get-tuple-element.8, bf16[3,2,4096]{2,1,0:T(2,128)(2,1)S(1)} %get-tuple-element.12, bf16[3,2,4096]{2,1,0:T(2,128)(2,1)S(1)} %get-tuple-element.11), kind=kLoop, calls=%fused_computation.1 | loop fusion | flops 589824 | bytes 491520 | tf_op jit(solution)/shard_map/transpose | solution.py:338
Async XLA Ops:
  10.8 9.1 %collective-permute-start = (bf16[3,2,4096]{2,1,0:T(2,128)(2,1)S(1)}, bf16[3,2,4096]{2,1,0:T(2,128)(2,1)S(1)}, u32[]{:S(2)}, u32[]{:S(2)}) collective-permute-start(bf16[3,2,4096]{2,1,0:T(2,128)(2,1)S(1)} %get-tuple-element.14), channel_id=1, source_target_pairs={{16,32},{48,64},{80,96},{112,128},{144,160},{176,192},{208,224},{2... | collective-permute-start | bytes 147464 | tf_op jit(solution)/shard_map/ppermute | solution.py:329

commit v4 on v2

--- a/solution.py
+++ b/solution.py
@@ -22,7 +22,6 @@
 HROWS = 8 * CHANNELS
 PROWS = 224
 BIG = -1e30
-UNROLL = 1
 
 f32 = jnp.float32
 bf16 = jnp.bfloat16
@@ -86,6 +85,7 @@
     yy, xx = lane >> 4, lane & 15
     low64 = iota((1, 128), 1) < 64
 
+    rs[...] = jnp.zeros_like(rs)
     for b in range(OWNED):
         vz[b] = jnp.zeros((2, 26 * VROWS, 128), f32)
         hx[b, 0:HROWS] = jnp.zeros((HROWS, LANES), bf16)
@@ -102,7 +102,31 @@
     td[...] = jnp.zeros_like(td)
     for copy in copies:
         copy.wait()
-
+    alive = tissue[0] + tissue[1]
+
+    work = functools.partial(
+        run, lane, yy, xx, low64, vol, w1, w2, wd, wup, wout, core, low_out, high_out,
+        t1, b2, td, w1big, w2big, wd3, wo, vs, vz, hx, fs, ps, px, ys, gs, us, zs, rs,
+    )
+
+    @pl.when(alive == 2)
+    def _():
+        work([0, 1])
+
+    @pl.when(alive == 1)
+    def _():
+        work([1 - tissue[0]])
+
+    @pl.when(alive == 0)
+    def _():
+        for ref in (core, low_out, high_out):
+            ref[...] = jnp.zeros_like(ref)
+
+
+def run(
+    lane, yy, xx, low64, vol, w1, w2, wd, wup, wout, core, low_out, high_out,
+    t1, b2, td, w1big, w2big, wd3, wo, vs, vz, hx, fs, ps, px, ys, gs, us, zs, rs, bricks,
+):
     for kz in range(3):
         for ky in range(3):
             at = kz * VROWS + ky * 4
@@ -172,8 +196,12 @@
                 vs[d, pl.ds(t * EXTENT + z, OWNED, stride=96), :] = vol[
                     :, at + 128 * d : at + 128 * d + 128
                 ].astype(f32)
-    sorted_cells = dot(jnp.concatenate([vs[0], vs[1]], axis=1).astype(bf16), sort)
-    for b in range(OWNED):
+    if len(bricks) == OWNED:
+        cells = [vs[d] for d in range(2)]
+    else:
+        cells = [vs[d, pl.ds(pl.multiple_of(bricks[0] * 96, 96), 96), :] for d in range(2)]
+    sorted_cells = dot(jnp.concatenate(cells, axis=1).astype(bf16), sort)
+    for b in range(len(bricks)):
         parts = [sorted_cells[b * 96 + t * 24 : b * 96 + t * 24 + 24] for t in range(4)]
         parities = swap_chunks(parts, low64)
         for p in range(4):
@@ -189,21 +217,15 @@
     def first(j):
         b, i = j // HALF, j % HALF
         at = i * (2 * VROWS)
-        if not isinstance(j, int):
-            at = pl.multiple_of(at, 2 * VROWS)
         near = [vz[b, d, pl.ds(at, 4 * VROWS), :] for d in range(2)]
         near = jnp.concatenate(near, axis=1).astype(bf16)
         out = jnp.maximum(dot(w1big[...], near), 0.0).astype(bf16)
         to = i * (2 * HROWS) + HROWS
-        if not isinstance(j, int):
-            to = pl.multiple_of(to, HROWS)
         hx[b, pl.ds(to, 2 * HROWS), :] = out
 
     def second(j):
         b, i = j // HALF, j % HALF
         at = i * (2 * HROWS)
-        if not isinstance(j, int):
-            at = pl.multiple_of(at, 2 * HROWS)
         out = dot(w2big[...], hx[b, pl.ds(at, 4 * HROWS), :])
         left = out[96:192] + along_x(out[288:384], -1, xx)
         right = out[192:288] + along_x(out[0:96], 1, xx)
@@ -238,14 +260,13 @@
     def project(j):
         b, i = j // HALF, j % HALF
         pred = jax.nn.sigmoid(dot(wo[...], zs[j]))
-        pred = jnp.where(tissue[b] == 1, pred, 0.0)
         for p in range(4):
             for d in range(2):
-                rs[p, d, pl.ds(i * 16 + b, 8, stride=2), :] = pred[
+                rs[p, d, pl.ds(i * 16 + bricks[b], 8, stride=2), :] = pred[
                     p * 8 : p * 8 + 8, 128 * d : 128 * d + 128
                 ]
 
-    units = OWNED * HALF
+    units = len(bricks) * HALF
 
     stages = ((second, 0), (first, 2), (coarse, -2), (lift, -5), (project, -7), (spread, -1), (gather, -4), (mix, -6))
     for j in range(-2, units + 7):
@@ -312,10 +333,15 @@
 def shards(volume, tissue, w_first, w_second, w_down, w_up, w_out):
     core, low, high = evaluate(volume, tissue, w_first, w_second, w_down, w_up, w_out)
     slabs = lax.axis_size("slab")
-    up = [(i, i + 1) for i in range(slabs - 1)]
-    down = [(i + 1, i) for i in range(slabs - 1)]
-    below = lax.ppermute(high, "slab", up)
-    above = lax.ppermute(low, "slab", down)
+    me = lax.axis_index("slab")
+    odd = (me % 2) == 1
+    across = [(i, i + 1) for i in range(1, slabs - 1, 2)] + [(i + 1, i) for i in range(1, slabs - 1, 2)]
+    chip = [[i, i + 1] for i in range(0, slabs, 2)]
+    two = lax.ppermute(jnp.where(odd, high, low), "slab", across)
+    one = lax.all_gather(jnp.where(odd, low, high), "slab", axis_index_groups=chip)
+    one = jnp.where(odd, one[0], one[1])
+    above = jnp.where(odd, two, one)
+    below = jnp.where(odd, one, two)
     rest = DEPTH * PLANE - MARGIN * PLANE
     total = core.astype(f32)
     total = total + jnp.pad(below.astype(f32), ((0, 0), (0, 0), (0, rest)))

time: 23.2 us -> 19.1 us (0.82)
  the two profiles are of different devices: /device:TPU:253 before, /device:TPU:245 now
where the time goes in v4:
time: 19.1 us; the launch traced here: 19 us
  starting transfers between devices  14.9 us (78%)
  blocking collectives  1.88 us (10%)
  Pallas kernels  1.14 us (6%)
  other arithmetic  1.06 us (6%)
    ppermute x1, starting transfers between devices, shards(): two = lax.ppermute(jnp.where(odd, high, low), 'slab', across)  14.9 us
    all_gather x1, blocking collectives, shards(): lax.all_gather(jnp.where(odd, low, high), 'slab', axis_index_groups=chip)  1.88 us
    pallas_call x1, Pallas kernels, evaluate(): pl.pallas_call(unet, out_shape=(jax.ShapeDtypeStruct((CLASSES, OWNED, DEP...  1.14 us
    transpose x1, other arithmetic, shards(): return jnp.transpose(total.astype(bf16), (1, 0, 2))  0.88 us
  transfers between devices with their start and end apart: 1, of which 0 were waited for; matrix products, arithmetic and copies ran while one was open for 0% of the time, Pallas kernels for 0%

profile of v4, /device:TPU:245, one launch (start us, length us, event | category | flops | bytes accessed | tf_op | source)
XLA Modules:
  0.0 19.0 jit_solution(6498112746179444948)
XLA Ops:
  0.0 1.1 %shard_map.73 = (bf16[3,2,16384]{2,1,0:T(2,128)(2,1)S(1)}, bf16[3,2,4096]{2,1,0:T(2,128)(2,1)S(1)}, bf16[3,2,4096]{2,1,0:T(2,128)(2,1)S(1)}) custom-call(s32[2]{0:T(128)} %refs_0_.1, bf16[2,24576]{1,0:T(2,128)(2,1)} %refs_1_.1, bf16[9,3,24]{2,1,0:T(4,128)(2,1)} %bitcast.13, bf16[27,24,24]{2,1,0:T(8,128)(2,1)} %bitcast.11, bf16[27,24,48]{2,1,0:T(8,128)(2,1)} %bitcast.12, ...), custom_call_target="tpu_custom_call" | custom-call | tf_op jit(solution)/shard_map/pallas_call | solution.py:301
  1.2 0.1 broadcast_select_fusion.4
  1.2 14.9 %collective-permute-start = (bf16[3,2,4096]{2,1,0:T(2,128)(2,1)S(1)}, bf16[3,2,4096]{2,1,0:T(2,128)(2,1)S(1)}, u32[]{:S(2)}, u32[]{:S(2)}) collective-permute-start(bf16[3,2,4096]{2,1,0:T(2,128)(2,1)S(1)} %get-tuple-element.14), channel_id=1, source_target_pairs={{16,32},{48,64},{80,96},{112,128},{144,160},{176,192},{208,224},{2... | collective-permute-start | bytes 147464 | tf_op jit(solution)/shard_map/ppermute | solution.py:340
  16.1 1.9 %all-gather = bf16[6,2,4096]{2,1,0:T(2,128)(2,1)S(1)} all-gather(bf16[3,2,4096]{2,1,0:T(2,128)(2,1)S(1)} %get-tuple-element.13), channel_id=2, replica_groups={{0,16},{32,48},{64,80},{96,112},{128,144},{160,176},{192,208},{224,240}..., dimensions={0}, use_global_device_ids=true | all-gather | bytes 147456 | tf_op jit(solution)/shard_map/all_gather | solution.py:341
  18.0 0.0 collective-permute-done
  18.0 0.1 broadcast_select_fusion.2
  18.1 0.9 %fusion = bf16[2,3,16384]{2,0,1:T(2,128)(2,1)} fusion(bf16[3,2,16384]{2,1,0:T(2,128)(2,1)S(1)} %get-tuple-element.8, bf16[3,2,4096]{2,1,0:T(2,128)(2,1)S(1)} %get-tuple-element.12, bf16[3,2,4096]{2,1,0:T(2,128)(2,1)S(1)} %get-tuple-element.11), kind=kLoop, calls=%fused_computation.1 | loop fusion | flops 589824 | bytes 491520 | tf_op jit(solution)/shard_map/transpose | solution.py:349
Async XLA Ops:
  1.2 16.8 %collective-permute-start = (bf16[3,2,4096]{2,1,0:T(2,128)(2,1)S(1)}, bf16[3,2,4096]{2,1,0:T(2,128)(2,1)S(1)}, u32[]{:S(2)}, u32[]{:S(2)}) collective-permute-start(bf16[3,2,4096]{2,1,0:T(2,128)(2,1)S(1)} %get-tuple-element.14), channel_id=1, source_target_pairs={{16,32},{48,64},{80,96},{112,128},{144,160},{176,192},{208,224},{2... | collective-permute-start | bytes 147464 | tf_op jit(solution)/shard_map/ppermute | solution.py:340

commit v5 on v4

--- a/solution.py
+++ b/solution.py
@@ -22,6 +22,7 @@
 HROWS = 8 * CHANNELS
 PROWS = 224
 BIG = -1e30
+ENDS = (6,)
 
 f32 = jnp.float32
 bf16 = jnp.bfloat16
@@ -266,27 +267,42 @@
                     p * 8 : p * 8 + 8, 128 * d : 128 * d + 128
                 ]
 
-    units = len(bricks) * HALF
-
-    stages = ((second, 0), (first, 2), (coarse, -2), (lift, -5), (project, -7), (spread, -1), (gather, -4), (mix, -6))
-    for j in range(-2, units + 7):
-        for stage, lag in stages:
-            if 0 <= j + lag < units:
-                stage(j + lag)
-
-    chunks = swap_chunks([jnp.concatenate([rs[p, 0], rs[p, 1]], axis=1) for p in range(4)], low64)
-    for t in range(4):
-        rows = dot(chunks[t].astype(bf16), unsort)
-        for z in range(EXTENT):
-            if z < MARGIN:
-                to, ref = z, low_out
-            elif z < MARGIN + DEPTH:
-                to, ref = z - MARGIN, core
-            else:
-                to, ref = z - MARGIN - DEPTH, high_out
-            for cls in range(CLASSES):
-                piece = rows[z * 8 + cls * 2 : z * 8 + cls * 2 + 2].astype(bf16)
-                ref[cls, :, to * PLANE + t * LANES : to * PLANE + t * LANES + LANES] = piece
+    def emit(first_layer, layers):
+        at = first_layer * 16
+        parts = [
+            jnp.concatenate([rs[p, d, at : at + layers * 16] for d in range(2)], axis=1)
+            for p in range(4)
+        ]
+        chunks = swap_chunks(parts, low64)
+        for t in range(4):
+            rows = dot(chunks[t].astype(bf16), unsort)
+            for z in range(2 * first_layer, 2 * (first_layer + layers)):
+                if z < MARGIN:
+                    to, ref = z, low_out
+                elif z < MARGIN + DEPTH:
+                    to, ref = z - MARGIN, core
+                else:
+                    to, ref = z - MARGIN - DEPTH, high_out
+                to = to * PLANE + t * LANES
+                for cls in range(CLASSES):
+                    r = (z - 2 * first_layer) * 8 + cls * 2
+                    ref[cls, :, to : to + LANES] = rows[r : r + 2].astype(bf16)
+
+    start = 0
+    for step in range(-2, HALF + 4):
+        for stage, lag in (
+            (second, 0), (coarse, -1), (lift, -3), (project, -4),
+            (first, 2), (mix, -3), (gather, -2), (spread, 0),
+        ):
+            if 0 <= step + lag < HALF:
+                for b in range(len(bricks)):
+                    stage(b * HALF + step + lag)
+        for end in ENDS:
+            if step == end + 3:
+                emit(start, end - start)
+                start = end
+    if start < HALF:
+        emit(start, HALF - start)
 
 
 VMEM = pl.BlockSpec(memory_space=pltpu.VMEM)

time: 19.1 us -> 18.7 us (0.979)
  the two profiles are of different devices: /device:TPU:245 before, /device:TPU:1 now
where the time goes in v5:
time: 18.7 us; the launch traced here: 18.6 us
  starting transfers between devices  12.2 us (65%)
  blocking collectives  4.12 us (22%)
  Pallas kernels  1.14 us (6%)
  other arithmetic  1.06 us (6%)
    ppermute x1, starting transfers between devices, shards(): two = lax.ppermute(jnp.where(odd, high, low), 'slab', across)  12.2 us
    all_gather x1, blocking collectives, shards(): lax.all_gather(jnp.where(odd, low, high), 'slab', axis_index_groups=chip)  4.12 us
    pallas_call x1, Pallas kernels, evaluate(): pl.pallas_call(unet, out_shape=(jax.ShapeDtypeStruct((CLASSES, OWNED, DEP...  1.14 us
    transpose x1, other arithmetic, shards(): return jnp.transpose(total.astype(bf16), (1, 0, 2))  0.88 us
  transfers between devices with their start and end apart: 1, of which 0 were waited for; matrix products, arithmetic and copies ran while one was open for 0% of the time, Pallas kernels for 0%

profile of v5, /device:TPU:1, one launch (start us, length us, event | category | flops | bytes accessed | tf_op | source)
XLA Modules:
  0.0 18.6 jit_solution(4680657914325434444)
XLA Ops:
  0.0 1.1 %shard_map.73 = (bf16[3,2,16384]{2,1,0:T(2,128)(2,1)S(1)}, bf16[3,2,4096]{2,1,0:T(2,128)(2,1)S(1)}, bf16[3,2,4096]{2,1,0:T(2,128)(2,1)S(1)}) custom-call(s32[2]{0:T(128)} %refs_0_.1, bf16[2,24576]{1,0:T(2,128)(2,1)} %refs_1_.1, bf16[9,3,24]{2,1,0:T(4,128)(2,1)} %bitcast.13, bf16[27,24,24]{2,1,0:T(8,128)(2,1)} %bitcast.11, bf16[27,24,48]{2,1,0:T(8,128)(2,1)} %bitcast.12, ...), custom_call_target="tpu_custom_call" | custom-call | tf_op jit(solution)/shard_map/pallas_call | solution.py:317
  1.2 0.1 broadcast_select_fusion.4
  1.2 12.2 %collective-permute-start = (bf16[3,2,4096]{2,1,0:T(2,128)(2,1)S(1)}, bf16[3,2,4096]{2,1,0:T(2,128)(2,1)S(1)}, u32[]{:S(2)}, u32[]{:S(2)}) collective-permute-start(bf16[3,2,4096]{2,1,0:T(2,128)(2,1)S(1)} %get-tuple-element.14), channel_id=1, source_target_pairs={{16,32},{48,64},{80,96},{112,128},{144,160},{176,192},{208,224},{2... | collective-permute-start | bytes 147464 | tf_op jit(solution)/shard_map/ppermute | solution.py:356
  13.5 4.1 %all-gather = bf16[6,2,4096]{2,1,0:T(2,128)(2,1)S(1)} all-gather(bf16[3,2,4096]{2,1,0:T(2,128)(2,1)S(1)} %get-tuple-element.13), channel_id=2, replica_groups={{0,16},{32,48},{64,80},{96,112},{128,144},{160,176},{192,208},{224,240}..., dimensions={0}, use_global_device_ids=true | all-gather | bytes 147456 | tf_op jit(solution)/shard_map/all_gather | solution.py:357
  17.6 0.0 collective-permute-done
  17.6 0.1 broadcast_select_fusion.2
  17.7 0.9 %fusion = bf16[2,3,16384]{2,0,1:T(2,128)(2,1)} fusion(bf16[3,2,16384]{2,1,0:T(2,128)(2,1)S(1)} %get-tuple-element.8, bf16[3,2,4096]{2,1,0:T(2,128)(2,1)S(1)} %get-tuple-element.12, bf16[3,2,4096]{2,1,0:T(2,128)(2,1)S(1)} %get-tuple-element.11), kind=kLoop, calls=%fused_computation.1 | loop fusion | flops 589824 | bytes 491520 | tf_op jit(solution)/shard_map/transpose | solution.py:365
Async XLA Ops:
  1.2 16.4 %collective-permute-start = (bf16[3,2,4096]{2,1,0:T(2,128)(2,1)S(1)}, bf16[3,2,4096]{2,1,0:T(2,128)(2,1)S(1)}, u32[]{:S(2)}, u32[]{:S(2)}) collective-permute-start(bf16[3,2,4096]{2,1,0:T(2,128)(2,1)S(1)} %get-tuple-element.14), channel_id=1, source_target_pairs={{16,32},{48,64},{80,96},{112,128},{144,160},{176,192},{208,224},{2... | collective-permute-start | bytes 147464 | tf_op jit(solution)/shard_map/ppermute | solution.py:356

commit v6 on v5

--- a/solution.py
+++ b/solution.py
@@ -22,7 +22,6 @@
 HROWS = 8 * CHANNELS
 PROWS = 224
 BIG = -1e30
-ENDS = (6,)
 
 f32 = jnp.float32
 bf16 = jnp.bfloat16
@@ -267,16 +266,12 @@
                     p * 8 : p * 8 + 8, 128 * d : 128 * d + 128
                 ]
 
-    def emit(first_layer, layers):
-        at = first_layer * 16
-        parts = [
-            jnp.concatenate([rs[p, d, at : at + layers * 16] for d in range(2)], axis=1)
-            for p in range(4)
-        ]
+    def emit():
+        parts = [jnp.concatenate([rs[p, d] for d in range(2)], axis=1) for p in range(4)]
         chunks = swap_chunks(parts, low64)
         for t in range(4):
             rows = dot(chunks[t].astype(bf16), unsort)
-            for z in range(2 * first_layer, 2 * (first_layer + layers)):
+            for z in range(EXTENT):
                 if z < MARGIN:
                     to, ref = z, low_out
                 elif z < MARGIN + DEPTH:
@@ -285,24 +280,21 @@
                     to, ref = z - MARGIN - DEPTH, high_out
                 to = to * PLANE + t * LANES
                 for cls in range(CLASSES):
-                    r = (z - 2 * first_layer) * 8 + cls * 2
-                    ref[cls, :, to : to + LANES] = rows[r : r + 2].astype(bf16)
-
-    start = 0
-    for step in range(-2, HALF + 4):
+                    piece = rows[z * 8 + cls * 2 : z * 8 + cls * 2 + 2].astype(bf16)
+                    ref[cls, :, to : to + LANES] = piece
+
+    half = HALF // 2
+    for step in range(-2, half + 4):
         for stage, lag in (
-            (second, 0), (coarse, -1), (lift, -3), (project, -4),
-            (first, 2), (mix, -3), (gather, -2), (spread, 0),
+            (second, 0), (first, 2), (coarse, -1), (lift, -3), (project, -4),
+            (mix, -3), (gather, -2), (spread, 0),
         ):
-            if 0 <= step + lag < HALF:
+            k = step + lag
+            if 0 <= k < half:
                 for b in range(len(bricks)):
-                    stage(b * HALF + step + lag)
-        for end in ENDS:
-            if step == end + 3:
-                emit(start, end - start)
-                start = end
-    if start < HALF:
-        emit(start, HALF - start)
+                    for i in (k, HALF - 1 - k):
+                        stage(b * HALF + i)
+    emit()
 
 
 VMEM = pl.BlockSpec(memory_space=pltpu.VMEM)

time: 18.7 us -> 17.9 us (0.957)
  the two profiles are of different devices: /device:TPU:1 before, /device:TPU:237 now
where the time goes in v6:
time: 17.9 us; the launch traced here: 17.7 us
  starting transfers between devices  8.24 us (46%)
  Pallas kernels  6.53 us (36%)
  blocking collectives  1.88 us (11%)
  other arithmetic  1.06 us (6%)
    ppermute x1, starting transfers between devices, shards(): two = lax.ppermute(jnp.where(odd, high, low), 'slab', across)  8.24 us
    pallas_call x1, Pallas kernels, evaluate(): pl.pallas_call(unet, out_shape=(jax.ShapeDtypeStruct((CLASSES, OWNED, DEP...  6.53 us
    all_gather x1, blocking collectives, shards(): lax.all_gather(jnp.where(odd, low, high), 'slab', axis_index_groups=chip)  1.88 us
    transpose x1, other arithmetic, shards(): return jnp.transpose(total.astype(bf16), (1, 0, 2))  0.88 us
  transfers between devices with their start and end apart: 1, of which 0 were waited for; matrix products, arithmetic and copies ran while one was open for 0% of the time, Pallas kernels for 0%

profile of v6, /device:TPU:237, one launch (start us, length us, event | category | flops | bytes accessed | tf_op | source)
XLA Modules:
  0.0 17.7 jit_solution(8084887906227400975)
XLA Ops:
  0.0 6.5 %shard_map.73 = (bf16[3,2,16384]{2,1,0:T(2,128)(2,1)S(1)}, bf16[3,2,4096]{2,1,0:T(2,128)(2,1)S(1)}, bf16[3,2,4096]{2,1,0:T(2,128)(2,1)S(1)}) custom-call(s32[2]{0:T(128)} %refs_0_.1, bf16[2,24576]{1,0:T(2,128)(2,1)} %refs_1_.1, bf16[9,3,24]{2,1,0:T(4,128)(2,1)} %bitcast.13, bf16[27,24,24]{2,1,0:T(8,128)(2,1)} %bitcast.11, bf16[27,24,48]{2,1,0:T(8,128)(2,1)} %bitcast.12, ...), custom_call_target="tpu_custom_call" | custom-call | tf_op jit(solution)/shard_map/pallas_call | solution.py:309
  6.5 0.1 broadcast_select_fusion.4
  6.6 8.2 %collective-permute-start = (bf16[3,2,4096]{2,1,0:T(2,128)(2,1)S(1)}, bf16[3,2,4096]{2,1,0:T(2,128)(2,1)S(1)}, u32[]{:S(2)}, u32[]{:S(2)}) collective-permute-start(bf16[3,2,4096]{2,1,0:T(2,128)(2,1)S(1)} %get-tuple-element.14), channel_id=1, source_target_pairs={{16,32},{48,64},{80,96},{112,128},{144,160},{176,192},{208,224},{2... | collective-permute-start | bytes 147464 | tf_op jit(solution)/shard_map/ppermute | solution.py:348
  14.9 1.9 %all-gather = bf16[6,2,4096]{2,1,0:T(2,128)(2,1)S(1)} all-gather(bf16[3,2,4096]{2,1,0:T(2,128)(2,1)S(1)} %get-tuple-element.13), channel_id=2, replica_groups={{0,16},{32,48},{64,80},{96,112},{128,144},{160,176},{192,208},{224,240}..., dimensions={0}, use_global_device_ids=true | all-gather | bytes 147456 | tf_op jit(solution)/shard_map/all_gather | solution.py:349
  16.8 0.0 collective-permute-done
  16.8 0.1 broadcast_select_fusion.2
  16.9 0.9 %fusion = bf16[2,3,16384]{2,0,1:T(2,128)(2,1)} fusion(bf16[3,2,16384]{2,1,0:T(2,128)(2,1)S(1)} %get-tuple-element.8, bf16[3,2,4096]{2,1,0:T(2,128)(2,1)S(1)} %get-tuple-element.12, bf16[3,2,4096]{2,1,0:T(2,128)(2,1)S(1)} %get-tuple-element.11), kind=kLoop, calls=%fused_computation.1 | loop fusion | flops 589824 | bytes 491520 | tf_op jit(solution)/shard_map/transpose | solution.py:357
Async XLA Ops:
  6.6 10.1 %collective-permute-start = (bf16[3,2,4096]{2,1,0:T(2,128)(2,1)S(1)}, bf16[3,2,4096]{2,1,0:T(2,128)(2,1)S(1)}, u32[]{:S(2)}, u32[]{:S(2)}) collective-permute-start(bf16[3,2,4096]{2,1,0:T(2,128)(2,1)S(1)} %get-tuple-element.14), channel_id=1, source_target_pairs={{16,32},{48,64},{80,96},{112,128},{144,160},{176,192},{208,224},{2... | collective-permute-start | bytes 147464 | tf_op jit(solution)/shard_map/ppermute | solution.py:348

commit v7 on v6

--- a/solution.py
+++ b/solution.py
@@ -347,13 +347,15 @@
     chip = [[i, i + 1] for i in range(0, slabs, 2)]
     two = lax.ppermute(jnp.where(odd, high, low), "slab", across)
     one = lax.all_gather(jnp.where(odd, low, high), "slab", axis_index_groups=chip)
-    one = jnp.where(odd, one[0], one[1])
-    above = jnp.where(odd, two, one)
-    below = jnp.where(odd, one, two)
     rest = DEPTH * PLANE - MARGIN * PLANE
+    lowest, highest = ((0, 0), (0, 0), (0, rest)), ((0, 0), (0, 0), (rest, 0))
+
+    def place(margin, at):
+        return jnp.pad(margin.astype(f32), at)
+
     total = core.astype(f32)
-    total = total + jnp.pad(below.astype(f32), ((0, 0), (0, 0), (0, rest)))
-    total = total + jnp.pad(above.astype(f32), ((0, 0), (0, 0), (rest, 0)))
+    total = total + jnp.where(odd, place(one[0], lowest), place(two, lowest))
+    total = total + jnp.where(odd, place(two, highest), place(one[1], highest))
     return jnp.transpose(total.astype(bf16), (1, 0, 2))
 
 

time: 17.9 us -> 17.9 us (level)
  no operation moved by 1% of the time
where the time goes in v7:
time: 17.9 us; the launch traced here: 17.8 us
  starting transfers between devices  8.24 us (46%)
  Pallas kernels  6.53 us (36%)
  blocking collectives  1.88 us (11%)
  other arithmetic  1.03 us (6%)
    ppermute x1, starting transfers between devices, shards(): two = lax.ppermute(jnp.where(odd, high, low), 'slab', across)  8.24 us
    pallas_call x1, Pallas kernels, evaluate(): pl.pallas_call(unet, out_shape=(jax.ShapeDtypeStruct((CLASSES, OWNED, DEP...  6.53 us
    all_gather x1, blocking collectives, shards(): lax.all_gather(jnp.where(odd, low, high), 'slab', axis_index_groups=chip)  1.88 us
    transpose x1, other arithmetic, shards(): return jnp.transpose(total.astype(bf16), (1, 0, 2))  0.91 us
  transfers between devices with their start and end apart: 1, of which 0 were waited for; matrix products, arithmetic and copies ran while one was open for 0% of the time, Pallas kernels for 0%

profile of v7, /device:TPU:237, one launch (start us, length us, event | category | flops | bytes accessed | tf_op | source)
XLA Modules:
  0.0 17.8 jit_solution(9616229737715321300)
XLA Ops:
  0.0 6.5 %shard_map.73 = (bf16[3,2,16384]{2,1,0:T(2,128)(2,1)S(1)}, bf16[3,2,4096]{2,1,0:T(2,128)(2,1)S(1)}, bf16[3,2,4096]{2,1,0:T(2,128)(2,1)S(1)}) custom-call(s32[2]{0:T(128)} %refs_0_.1, bf16[2,24576]{1,0:T(2,128)(2,1)} %refs_1_.1, bf16[9,3,24]{2,1,0:T(4,128)(2,1)} %bitcast.13, bf16[27,24,24]{2,1,0:T(8,128)(2,1)} %bitcast.11, bf16[27,24,48]{2,1,0:T(8,128)(2,1)} %bitcast.12, ...), custom_call_target="tpu_custom_call" | custom-call | tf_op jit(solution)/shard_map/pallas_call | solution.py:309
  6.5 0.1 broadcast_select_fusion
  6.6 8.2 %collective-permute-start = (bf16[3,2,4096]{2,1,0:T(2,128)(2,1)S(1)}, bf16[3,2,4096]{2,1,0:T(2,128)(2,1)S(1)}, u32[]{:S(2)}, u32[]{:S(2)}) collective-permute-start(bf16[3,2,4096]{2,1,0:T(2,128)(2,1)S(1)} %get-tuple-element.13), channel_id=1, source_target_pairs={{16,32},{48,64},{80,96},{112,128},{144,160},{176,192},{208,224},{2... | collective-permute-start | bytes 147464 | tf_op jit(solution)/shard_map/ppermute | solution.py:348
  14.9 1.9 %all-gather = bf16[6,2,4096]{2,1,0:T(2,128)(2,1)S(1)} all-gather(bf16[3,2,4096]{2,1,0:T(2,128)(2,1)S(1)} %get-tuple-element.14), channel_id=2, replica_groups={{0,16},{32,48},{64,80},{96,112},{128,144},{160,176},{192,208},{224,240}..., dimensions={0}, use_global_device_ids=true | all-gather | bytes 147456 | tf_op jit(solution)/shard_map/all_gather | solution.py:349
  16.8 0.1 fusion.1
  16.8 0.0 collective-permute-done
  16.9 0.9 %fusion = bf16[2,3,16384]{2,0,1:T(2,128)(2,1)} fusion(bf16[3,2,4096]{2,1,0:T(2,128)(2,1)S(1)} %get-tuple-element.12, f32[3,2,4096]{2,1,0:T(2,128)S(1)} %convert_element_type.26, bf16[3,2,4096]{2,1,0:T(2,128)(2,1)S(1)} %get-tuple-element.11, pred[]{:T(512)S(6)} %eq.5, bf16[3,2,16384]{2,1,0:T(2,128)(2,1)S(1)} %get-tuple-element.8), kind=kLoop, calls=%fused_computation.1 | loop fusion | flops 786432 | bytes 589825 | tf_op jit(solution)/shard_map/transpose | solution.py:359
  (1 shorter events, 0.0 us)
Async XLA Ops:
  6.6 10.2 %collective-permute-start = (bf16[3,2,4096]{2,1,0:T(2,128)(2,1)S(1)}, bf16[3,2,4096]{2,1,0:T(2,128)(2,1)S(1)}, u32[]{:S(2)}, u32[]{:S(2)}) collective-permute-start(bf16[3,2,4096]{2,1,0:T(2,128)(2,1)S(1)} %get-tuple-element.13), channel_id=1, source_target_pairs={{16,32},{48,64},{80,96},{112,128},{144,160},{176,192},{208,224},{2... | collective-permute-start | bytes 147464 | tf_op jit(solution)/shard_map/ppermute | solution.py:348
